TPU v7x, 32 devices: a whole 2x2x4 slice. The times are simulated.
32 devices in a mesh: groups: 2 (over y), gx: 4 (over z), gy: 2 (over x), col: 2 (over core).
Axes of the slice: x: 2, y: 2, z: 4, core: 2. Of those that a mesh axis runs over, the one named last changes fastest.
Arguments:
- state_in: bfloat16 [64, 2048, 2048], P(('groups', 'col'), 'gx', 'gy'), parts along dimension 0, may hold values from -6 to 6
- tile_class: int32 [256, 128], P(('groups', 'gx'), 'gy'), parts along dimension 0, may hold values from 0 to 7
- class_bias: float32 [8, 32], replicated, may hold values from -4 to 4
- w_point: bfloat16 [32, 32], replicated, may hold values from -1 to 1
- spec_weight: bfloat16 [2, 32, 32, 128, 128], P(None, None, 'col', 'gx', 'gy'), may hold values from -0.75 to 0.75
- grad_out: bfloat16 [64, 2048, 2048], P(('groups', 'col'), 'gx', 'gy'), parts along dimension 0, may hold values from -6 to 6
Outputs:
- act_out: bfloat16 [64, 2048, 2048], P(('groups', 'col'), 'gx', 'gy'), parts along dimension 0
- grad_in: bfloat16 [64, 2048, 2048], P(('groups', 'col'), 'gx', 'gy'), parts along dimension 0
- grad_spec: float32 [4, 32, 32, 128, 128], P('groups', None, 'col', 'gx', 'gy'), parts along dimension 0
- grad_point: float32 [64, 32], P(('groups', 'col')), parts along dimension 0
- grad_bias: float32 [16, 32], P('groups', 'col'), parts along dimension 0
There are 2 independent parts, one for each index of `groups`. A program takes and returns all parts, laid end to end along the dimension named above; an argument that names none is the same for every part. Nothing has to cross between parts.
Inputs may be any that keep to these rules, and one draw needn't show every extreme that they name: `tile_class`: bathymetry class of each 16 x 16 tile of cells.
All inputs are finite; a program needn't handle non-finite values.
Results may differ from a plain program's by a relative error of at most 0.015.
Values may be sent and summed in bfloat16 or wider, within the bound.
A program may use at most 640 MiB of HBM per device.

v0:
```python
import math

import jax
import jax.numpy as jnp
from jax import lax
from jax.sharding import PartitionSpec as P

NX = 2048
NY = 2048
MX = 128
MY = 128
TILE = 16
NCLASS = 8


root_half = 0.7071067811865476
inv_root_tau = 0.3989422804014327


def y_forward_table(offset, length):
    freq_y = jnp.arange(MY, dtype=jnp.int32)
    points = offset + jnp.arange(length, dtype=jnp.int32)
    angles = (points[:, None] * freq_y[None, :] % NY).astype(jnp.float32) * (2.0 * math.pi / NY)
    return jnp.stack([jnp.cos(angles), -jnp.sin(angles)]).astype(jnp.bfloat16)


def y_inverse_table(offset, length):
    freq_y = jnp.arange(MY, dtype=jnp.int32)
    points = offset + jnp.arange(length, dtype=jnp.int32)
    angles = (freq_y[:, None] * points[None, :] % NY).astype(jnp.float32) * (2.0 * math.pi / NY)
    weight_k = jnp.where(freq_y == 0, 1.0, 2.0).astype(jnp.float32)[:, None]
    return jnp.stack([weight_k * jnp.cos(angles), -weight_k * jnp.sin(angles)]).astype(jnp.bfloat16)


def x_tables(offset, length):
    freq_x = jnp.arange(MX, dtype=jnp.int32)
    signed_x = jnp.where(freq_x < MX // 2, freq_x, freq_x - MX)
    points = offset + jnp.arange(length, dtype=jnp.int32)
    angles = (signed_x[:, None] * points[None, :] % NX).astype(jnp.float32) * (2.0 * math.pi / NX)
    cos_part = jnp.cos(angles)
    sin_part = jnp.sin(angles)
    x_fwd = jnp.stack([jnp.stack([cos_part, -sin_part]), jnp.stack([sin_part, cos_part])]).astype(
        jnp.bfloat16
    )
    x_inv = jnp.stack([jnp.stack([cos_part, sin_part]), jnp.stack([-sin_part, cos_part])]).astype(
        jnp.bfloat16
    )
    return (x_fwd, x_inv)


def mix_modes(weight, spectrum):
    high = lax.Precision.HIGHEST
    real_part = jnp.einsum("iokm,ikm->okm", weight[0], spectrum[0], precision=high) - jnp.einsum(
        "iokm,ikm->okm", weight[1], spectrum[1], precision=high
    )
    imag_part = jnp.einsum("iokm,ikm->okm", weight[0], spectrum[1], precision=high) + jnp.einsum(
        "iokm,ikm->okm", weight[1], spectrum[0], precision=high
    )
    return jnp.stack([real_part, imag_part])


def back_mix(weight, grad_modes):
    high = lax.Precision.HIGHEST
    real_part = jnp.einsum("iokm,okm->ikm", weight[0], grad_modes[0], precision=high) + jnp.einsum(
        "iokm,okm->ikm", weight[1], grad_modes[1], precision=high
    )
    imag_part = jnp.einsum("iokm,okm->ikm", weight[0], grad_modes[1], precision=high) - jnp.einsum(
        "iokm,okm->ikm", weight[1], grad_modes[0], precision=high
    )
    return jnp.stack([real_part, imag_part])


def weight_grad(spectrum, grad_modes):
    real_part = jnp.einsum("ikm,okm->iokm", spectrum[0], grad_modes[0]) + jnp.einsum(
        "ikm,okm->iokm", spectrum[1], grad_modes[1]
    )
    imag_part = jnp.einsum("ikm,okm->iokm", spectrum[0], grad_modes[1]) - jnp.einsum(
        "ikm,okm->iokm", spectrum[1], grad_modes[0]
    )
    return jnp.stack([real_part, imag_part])


def on_device(state_in, tile_class, class_bias, w_point, spec_weight, grad_out):
    own_chan, row_count, col_count = state_in.shape
    gx_index = lax.axis_index("gx")
    gy_index = lax.axis_index("gy")
    col_index = lax.axis_index("col")
    scale_fwd = 1.0 / math.sqrt(NX * NY)
    scale_inv = 1.0 / math.sqrt(2.0 * MX * MY)
    y_fwd = y_forward_table(gy_index * col_count, col_count)
    y_inv = y_inverse_table(gy_index * col_count, col_count)
    fwd_all, inv_all = x_tables(0, NX)
    fwd_own, inv_own = x_tables(gx_index * row_count, row_count)
    state_all = lax.all_gather(state_in, "col", axis=0, tiled=True)
    w_rows = lax.dynamic_slice_in_dim(w_point, col_index * own_chan, own_chan, 0)
    w_cols = lax.dynamic_slice_in_dim(w_point, col_index * own_chan, own_chan, 1)
    point_mix = jnp.einsum("oi,ixy->oxy", w_rows, state_all, preferred_element_type=jnp.float32)
    row_spec = jnp.einsum(
        "cxy,tyk->tckx", state_in, y_fwd, preferred_element_type=jnp.float32
    ).astype(jnp.bfloat16)
    row_full = lax.all_to_all(row_spec, "gx", split_axis=2, concat_axis=3, tiled=True)
    col_terms = jnp.einsum("rckx,rtmx->tckm", row_full, fwd_all, preferred_element_type=jnp.float32)
    spectrum = lax.psum_scatter(col_terms, "gy", scatter_dimension=3, tiled=True) * scale_fwd
    spec_all = lax.all_gather(spectrum, "col", axis=1, tiled=True)
    weight_f = spec_weight.astype(jnp.float32)
    mixed = mix_modes(weight_f, spec_all).astype(jnp.bfloat16)
    mixed_kx = lax.all_gather(mixed, "gy", axis=3, tiled=True)
    mixed_all = lax.all_gather(mixed_kx, "gx", axis=2, tiled=True)
    space_rows = jnp.einsum(
        "rokm,rtmx->tokx", mixed_all, inv_own, preferred_element_type=jnp.float32
    ).astype(jnp.bfloat16)
    spectral = scale_inv * jnp.einsum(
        "tokx,tky->oxy", space_rows, y_inv, preferred_element_type=jnp.float32
    )
    tile_rows = row_count // TILE
    tile_cols = col_count // TILE
    one_hot = (tile_class[:, :, None] == jnp.arange(NCLASS, dtype=jnp.int32)).astype(jnp.float32)
    bias_own = lax.dynamic_slice_in_dim(class_bias, col_index * own_chan, own_chan, 1)
    tile_bias = jnp.einsum("abn,no->oab", one_hot, bias_own)
    summed = (point_mix + spectral).reshape(own_chan, tile_rows, TILE, tile_cols, TILE)
    pre_act = (summed + tile_bias[:, :, None, :, None]).reshape(own_chan, row_count, col_count)
    normal_cdf = 0.5 * (1.0 + jax.scipy.special.erf(pre_act * root_half))
    act_out = (pre_act * normal_cdf).astype(jnp.bfloat16)
    gelu_slope = normal_cdf + pre_act * jnp.exp(-0.5 * pre_act * pre_act) * inv_root_tau
    grad_pre = (grad_out.astype(jnp.float32) * gelu_slope).astype(jnp.bfloat16)
    grad_all = lax.all_gather(grad_pre, "col", axis=0, tiled=True)
    point_grad = scale_fwd * jnp.einsum(
        "oxy,ixy->oi", grad_pre, state_all, preferred_element_type=jnp.float32
    )
    tile_sums = (
        grad_pre.astype(jnp.float32)
        .reshape(own_chan, tile_rows, TILE, tile_cols, TILE)
        .sum(axis=(2, 4))
    )
    bias_grad = scale_fwd * jnp.einsum("abn,oab->no", one_hot, tile_sums)
    point_grad, bias_grad = lax.psum((point_grad, bias_grad), ("gx", "gy"))
    grad_rows = (
        scale_inv * jnp.einsum("oxy,tky->tokx", grad_pre, y_inv, preferred_element_type=jnp.float32)
    ).astype(jnp.bfloat16)
    row_terms = jnp.einsum(
        "tokx,rtmx->rokm", grad_rows, inv_own, preferred_element_type=jnp.float32
    )
    row_sums = lax.psum_scatter(row_terms, "gx", scatter_dimension=2, tiled=True)
    grad_modes = lax.psum_scatter(row_sums, "gy", scatter_dimension=3, tiled=True)
    spec_grad = weight_grad(spec_all, grad_modes)
    input_terms = back_mix(weight_f, grad_modes)
    input_modes = lax.psum_scatter(input_terms, "col", scatter_dimension=1, tiled=True).astype(
        jnp.bfloat16
    )
    input_kx = lax.all_gather(input_modes, "gy", axis=3, tiled=True)
    input_all = lax.all_gather(input_kx, "gx", axis=2, tiled=True)
    grad_space = (
        scale_fwd
        * jnp.einsum("tckm,rtmx->rckx", input_all, fwd_own, preferred_element_type=jnp.float32)
    ).astype(jnp.bfloat16)
    point_back = jnp.einsum("oi,oxy->ixy", w_cols, grad_all, preferred_element_type=jnp.float32)
    spectral_back = jnp.einsum(
        "rckx,ryk->cxy", grad_space, y_fwd, preferred_element_type=jnp.float32
    )
    grad_in = (point_back + spectral_back).astype(jnp.bfloat16)
    return (act_out, grad_in, spec_grad, point_grad, bias_grad)


def solution(mesh):
    return jax.shard_map(
        on_device,
        mesh=mesh,
        in_specs=(
            P(("groups", "col"), "gx", "gy"),
            P(("groups", "gx"), "gy"),
            P(),
            P(),
            P(None, None, "col", "gx", "gy"),
            P(("groups", "col"), "gx", "gy"),
        ),
        out_specs=(
            P(("groups", "col"), "gx", "gy"),
            P(("groups", "col"), "gx", "gy"),
            P("groups", None, "col", "gx", "gy"),
            P(("groups", "col"), None),
            P("groups", "col"),
        ),
        check_vma=False,
    )
```

profile of v0, /device:TPU:0, one launch (start us, length us, event | category | flops | bytes accessed | tf_op | source)
XLA Modules:
  0.0 1171.0 jit_solution(9284038670558054245)
XLA Ops:
  7.2 2.2 cosine_convert_fusion.1
  9.5 8.4 convert_bitcast_fusion
  17.8 4.4 copy.63
  22.2 6.3 all-to-all-start
  28.9 4.9 negate_convert_fusion
  34.0 88.0 %all-to-all-done = bf16[2,16,128,512]{3,1,0,2:T(8,128)(2,1)} async-done(((bf16[2,16,128,512]{3,1,0,2:T(8,128)(2,1)}), bf16[2,16,128,512]{3,1,0,2:T(8,128)(2,1)}, u32[]{:S(2)}, u32[]{:S(2)}) %all-to-all-start) | async-done | bytes 4194336 | tf_op jit(solution)/shard_map/all_to_all | solution.py:101
  122.0 7.4 copy.198
  129.4 7.7 reshape.595
  137.2 3.5 fusion.44
  140.6 1.8 copy.163
  142.5 1.8 reshape.632
  144.3 13.8 %reduce-scatter.13.cloned.1.call-done = f32[64,1024]{1,0:T(8,128)} async-done(((f32[128,1024]{1,0:T(8,128)}), f32[64,1024]{1,0:T(8,128)}) %reduce-scatter.13.cloned.1.call-update) | async-done | bytes 262160
  160.1 3.1 all_gather.22
  164.0 6.3 fusion.15
  171.3 14.6 %all_gather.23 = bf16[2,16,32,128]{2,1,0,3:T(8,128)(2,1)S(1)} all-gather(bf16[2,16,32,64]{2,1,0,3:T(8,128)(2,1)S(1)} %copy.65), channel_id=1, replica_groups=mesh['groups'=2,'gx'=4,'gy'=2,'col'=2] {'gy'}, dimensions={3}, use_global_device_ids=true | all-gather | bytes 393216 | tf_op jit(solution)/shard_map/all_gather | solution.py:107
  185.9 1.8 copy.66
  187.7 18.7 %copy.60 = bf16[16,512,1024]{2,0,1:T(8,128)(2,1)} copy(bf16[16,512,1024]{2,1,0:T(8,128)(2,1)} %param.6) | data formatting | bytes 33554432 | tf_op args[0]
  207.6 99.5 %add.186 = f32[16,32,16,64,16]{4,3,2,1,0:T(8,128)} broadcast(f32[16,32,64]{2,1,0:T(8,128)S(1)} %copy.68), dimensions={0,1,3} | broadcast | bytes 33685504 | tf_op jit(solution)/shard_map/add | solution.py:121
  307.1 211.5 %add.187 = f32[16,512,1024]{2,1,0:T(8,128)} reshape(f32[16,32,16,64,16]{4,3,2,1,0:T(8,128)} %add.186) | data formatting | bytes 67108864 | tf_op jit(solution)/shard_map/add | solution.py:121
  520.8 2.2 multiply_convert_fusion.3
  523.0 2.5 fusion.25
  525.5 15.9 %fusion.29 = f32[16,512,1024,1]{2,0,3,1:T(8,128)} fusion(bf16[2,16,128,512]{2,3,0,1:T(8,128)(2,1)S(1)} %fusion.25, bf16[1,128,1024]{2,1,0:T(8,128)(2,1)S(1)} %get-tuple-element.60, bf16[1,128,1024]{2,1,0:T(8,128)(2,1)S(1)} %get-tuple-element.59), kind=kOutput, calls=%fused_computation.47 | convolution fusion | flops 4295229440 | bytes 38273024 | tf_op jit(solution)/shard_map/tokx,tky->oxy/dot_general | solution.py:112
  541.4 60.1 %fusion.5 = (bf16[16,512,1024]{2,0,1:T(8,128)(2,1)}, bf16[16,512,1024]{2,0,1:T(8,128)(2,1)}) fusion(bf16[16,512,1024]{2,1,0:T(8,128)(2,1)} %param.11, f32[16,512,1024]{2,1,0:T(8,128)} %add.187, f32[16,512,1024,1]{2,0,3,1:T(8,128)} %fusion.29, bf16[32,512,1024]{2,0,1:T(8,128)(2,1)} %all-gather.5.cloned.1.call-done, bf16[32,32]{1,0:T(8,128)(2,1)S(1)} %copy-done, ...), kind=kOutput, calls=%fused_computation.6 | convolution fusion | flops 671088640 | bytes 150999040 | tf_op jit(solution)/shard_map/oi,ixy->oxy/dot_general | solution.py:97
  601.5 33.5 %fusion.37 = f32[2,16,128,128]{2,3,1,0:T(8,128)S(1)} fusion(bf16[16,512,1024,1]{2,0,1,3:T(8,128)(2,1)} %bitcast.235, bf16[1,128,1024]{2,1,0:T(8,128)(2,1)S(1)} %get-tuple-element.60, bf16[1,128,1024]{2,1,0:T(8,128)(2,1)S(1)} %get-tuple-element.59, bf16[1,2,128,512]{2,3,0,1:T(8,128)(2,1)S(1)} %get-tuple-element.54, ...), kind=kOutput, calls=%fused_computation.56 | convolution fusion | flops 5374214144 | bytes 19922944 | tf_op jit(solution)/shard_map/tokx,rtmx->rokm/dot_general | solution.py:140
  634.9 2.0 copy.74
  637.0 44.0 %reduce-scatter.9.cloned.1.call-done = f32[2,16,32,128]{3,1,0,2:T(8,128)} async-done(((f32[2,16,128,128]{3,1,0,2:T(8,128)}), f32[2,16,32,128]{3,1,0,2:T(8,128)}) %reduce-scatter.9.cloned.1.call-update) | async-done | bytes 524304 | tf_op jit(solution)/shard_map/reduce_scatter | solution.py:143
  681.0 5.6 copy.165
  686.6 8.7 reshape.634
  695.4 14.0 %reduce-scatter.15.cloned.1.call-done = f32[64,1024]{1,0:T(8,128)} async-done(((f32[128,1024]{1,0:T(8,128)}), f32[64,1024]{1,0:T(8,128)}) %reduce-scatter.15.cloned.1.call-update) | async-done | bytes 262160
  709.3 3.7 reshape.635
  713.1 3.7 fusion.107
  716.8 2.3 copy.177
  719.1 2.3 copy.175
  721.5 14.4 %add_bitcast_fusion = (f32[1,32,16,32,64]{4,3,2,1,0:T(8,128)}, f32[1,32,16,32,64]{4,3,2,1,0:T(8,128)}, f32[32,64,32]{1,0,2:T(8,128)S(1)}, f32[32,64,32]{1,0,2:T(...) fusion(f32[32,64,16]{1,0,2:T(8,128)S(1)} %bitcast.241, f32[32,64,16]{1,0,2:T(8,128)S(1)} %bitcast.242, ...), kind=kLoop, calls=%fused_computation.39 | loop fusion | flops 16515072 | bytes 14417920 | tf_op jit(solution)/shard_map/stack | solution.py:80
  737.5 8.4 reduce-scatter.11.cloned.1.call-done
  747.8 14.8 %all_gather.26 = bf16[2,16,32,128]{2,1,0,3:T(8,128)(2,1)S(1)} all-gather(bf16[2,16,32,64]{2,1,0,3:T(8,128)(2,1)S(1)} %copy.75), channel_id=1, replica_groups=mesh['groups'=2,'gx'=4,'gy'=2,'col'=2] {'gy'}, dimensions={3}, use_global_device_ids=true | all-gather | bytes 393216 | tf_op jit(solution)/shard_map/all_gather | solution.py:150
  762.6 1.8 copy.76
  765.1 21.9 %copy.81 = f32[16,512,1024]{2,1,0:T(8,128)} copy(bf16[16,512,1024]{2,0,1:T(8,128)(2,1)} %get-tuple-element.39) | data formatting | bytes 50331648 | tf_op jit(solution)/shard_map/reshape | solution.py:132
  787.0 19.3 %copy.83 = bf16[16,512,1024]{2,1,0:T(8,128)(2,1)} copy(bf16[16,512,1024]{2,0,1:T(8,128)(2,1)} %get-tuple-element.40) | data formatting | bytes 33554432
  806.4 142.7 %reshape.590 = f32[16,32,16,64,16]{4,3,2,1,0:T(8,128)} reshape(f32[16,512,1024]{2,1,0:T(8,128)} %copy.81) | data formatting | bytes 67108864 | tf_op jit(solution)/shard_map/reshape | solution.py:132
  949.1 80.2 %reduce_sum.9 = bf16[16,32,64]{2,1,0:T(8,128)(2,1)S(1)} reduce(f32[16,32,16,64,16]{4,3,2,1,0:T(8,128)} %reshape.590, f32[]{:T(128)} %constant.92.clone.1), dimensions={2,4}, to_apply=%region_5.6 | reduce | flops 8355840 | bytes 33619972 | tf_op jit(solution)/shard_map/reduce_sum | solution.py:133
  1029.5 18.6 %fusion.45 = f32[16,32]{1,0:T(8,128)S(1)} fusion(bf16[16,512,1024]{2,0,1:T(8,128)(2,1)} %get-tuple-element.39, bf16[32,512,1024]{2,0,1:T(8,128)(2,1)} %all-gather.5.cloned.1.call-done), kind=kOutput, calls=%fused_computation.62 | convolution fusion | flops 536871424 | bytes 50333696 | tf_op jit(solution)/shard_map/oxy,ixy->oi/dot_general | solution.py:127
  1048.1 37.7 %all-reduce = (f32[16,32]{1,0:T(8,128)}, f32[8,16]{1,0:T(8,128)}) all-reduce(f32[16,32]{1,0:T(8,128)S(1)} %fusion.45, f32[8,16]{1,0:T(8,128)S(1)} %fusion.46), channel_id=1, replica_groups=mesh['groups'=2,'gx'=4,'gy'=2,'col'=2] {'gx','gy'}, use_global_device_ids=true, to_apply=%region_4.5 | all-reduce | flops 640 | bytes 5120 | tf_op jit(solution)/shard_map/psum | solution.py:136
  1085.8 12.3 %pad_maximum_fusion = f32[2,32,16,32,64]{4,3,2,1,0:T(8,128)} fusion(f32[1,32,16,32,64]{4,3,2,1,0:T(8,128)} %get-tuple-element.44, f32[1,32,16,32,64]{4,3,2,1,0:T(8,128)} %get-tuple-element.43), kind=kLoop, calls=%fused_computation.14 | loop fusion | flops 2097152 | bytes 16777216 | tf_op jit(solution)/shard_map/stack | solution.py:80
  1098.2 2.5 fusion.26
  1100.7 15.9 %fusion.27 = f32[16,512,1024,1]{2,0,3,1:T(8,128)} fusion(bf16[2,16,128,512]{2,3,0,1:T(8,128)(2,1)S(1)} %fusion.26, bf16[1,1024,128]{1,2,0:T(8,128)(2,1)S(1)} %copy-done.8, bf16[1,1024,128]{1,2,0:T(8,128)(2,1)S(1)} %copy-done.6), kind=kOutput, calls=%fused_computation.45 | convolution fusion | flops 4295229440 | bytes 38273024 | tf_op jit(solution)/shard_map/rckx,ryk->cxy/dot_general | solution.py:157
  1116.6 28.6 %fusion.6 = bf16[16,512,1024]{2,0,1:T(8,128)(2,1)} fusion(f32[16,512,1024,1]{2,0,3,1:T(8,128)} %fusion.27, bf16[32,512,1024]{2,0,1:T(8,128)(2,1)} %all-gather.9.cloned.1.call-done, bf16[32,32]{1,0:T(8,128)(2,1)S(1)} %copy-done, s32[]{:T(128)S(6)} %select_n.118), kind=kOutput, calls=%fused_computation.8 | convolution fusion | flops 553648128 | bytes 83888128 | tf_op jit(solution)/shard_map/oi,oxy->ixy/dot_general | solution.py:156
  1145.2 18.7 %copy.84 = bf16[16,512,1024]{2,1,0:T(8,128)(2,1)} copy(bf16[16,512,1024]{2,0,1:T(8,128)(2,1)} %fusion.6) | data formatting | bytes 33554432
  (78 shorter events, 12.0 us)
Async XLA Ops:
  7.2 534.2 %copy-start = (bf16[32,32]{1,0:T(8,128)(2,1)S(1)}, bf16[32,32]{1,0:T(8,128)(2,1)}, u32[]{:S(2)}) copy-start(bf16[32,32]{1,0:T(8,128)(2,1)} %param.9) | copy-start | bytes 6148
  7.2 2.3 copy-start.11
  9.4 8.4 copy-start.5
  9.4 8.4 copy-start.7
  22.2 99.7 %all-to-all-start = ((bf16[2,16,128,512]{3,1,0,2:T(8,128)(2,1)}), bf16[2,16,128,512]{3,1,0,2:T(8,128)(2,1)}, u32[]{:S(2)}, u32[]{:S(2)}) async-start(bf16[2,16,128,512]{3,1,0,2:T(8,128)(2,1)} %copy.63), calls=%async_computation | async-start | bytes 8388608 | tf_op jit(solution)/shard_map/all_to_all | solution.py:101
  28.6 129.6 %reduce-scatter.13.cloned.1.call-start = ((), (), s32[]{:S(2)}) async-start(), calls=%async_computation.11 | async-start | bytes 786432
  28.9 4.9 copy-start.15
  144.2 378.7 %all-gather.7.cloned.1.call-start = ((), (), s32[]{:S(2)}) async-start(), calls=%async_computation.6 | async-start | bytes 1310720 | tf_op jit(solution)/shard_map/all_gather | solution.py:108
  163.2 0.8 copy-start.1
  163.2 7.1 copy-start.3
  187.7 353.7 %all-gather.5.cloned.1.call-start = ((), (), s32[]{:S(2)}) async-start(), calls=%async_computation.5 | async-start | bytes 50331648 | tf_op jit(solution)/shard_map/all_gather | solution.py:94
  206.5 0.7 copy-start.13
  206.5 0.7 copy-start.17
  206.5 474.5 %reduce-scatter.9.cloned.1.call-start = ((), (), s32[]{:S(2)}) async-start(), calls=%async_computation.8 | async-start | bytes 2621440 | tf_op jit(solution)/shard_map/reduce_scatter | solution.py:143
  307.1 211.5 %copy-start.16 = (s32[128]{0:T(128)S(1)}, s32[128]{0:T(128)}, u32[]{:S(2)}) copy-start(s32[128]{0:T(128)} %copy-done.15) | copy-start | bytes 1540
  307.1 213.7 %copy-start.12 = (s32[1024]{0:T(1024)S(1)}, s32[1024]{0:T(1024)}, u32[]{:S(2)}) copy-start(s32[1024]{0:T(1024)} %copy-done.11) | copy-start | bytes 12292
  636.9 72.4 %reduce-scatter.15.cloned.1.call-start = ((), (), s32[]{:S(2)}) async-start(), calls=%async_computation.12 | async-start | bytes 786432
  686.6 34.9 %copy-start.2 = (f32[32,64,32]{1,0,2:T(8,128)S(1)}, f32[32,64,32]{1,0,2:T(8,128)}, u32[]{:S(2)}) copy-start(f32[32,64,32]{1,0,2:T(8,128)} %copy-done.1) | copy-start | bytes 786436
  686.6 34.9 %copy-start.4 = (f32[32,64,32]{1,0,2:T(8,128)S(1)}, f32[32,64,32]{1,0,2:T(8,128)}, u32[]{:S(2)}) copy-start(f32[32,64,32]{1,0,2:T(8,128)} %copy-done.3) | copy-start | bytes 786436
  695.3 50.6 %reduce-scatter.11.cloned.1.call-start = ((), (), s32[]{:S(2)}) async-start(), calls=%async_computation.9 | async-start | bytes 1572864 | tf_op jit(solution)/shard_map/reduce_scatter | solution.py:147
  737.2 361.0 %all-gather.11.cloned.1.call-start = ((), (), s32[]{:S(2)}) async-start(), calls=%async_computation.10 | async-start | bytes 1310720 | tf_op jit(solution)/shard_map/all_gather | solution.py:151
  764.4 352.2 %all-gather.9.cloned.1.call-start = ((), (), s32[]{:S(2)}) async-start(), calls=%async_computation.7 | async-start | bytes 50331648 | tf_op jit(solution)/shard_map/all_gather | solution.py:126
  949.1 80.2 %copy-start.14 = (s32[32,64]{1,0:T(8,128)S(1)}, s32[32,64]{1,0:T(8,128)}, u32[]{:S(2)}) copy-start(s32[32,64]{1,0:T(8,128)} %param.7) | copy-start | bytes 24580
  1085.8 12.3 %copy-start.9 = (bf16[1,2,128,512]{2,3,1,0:T(8,128)(2,1)S(1)}, bf16[1,2,128,512]{2,3,1,0:T(8,128)(2,1)}, u32[]{:S(2)}) copy-start(bf16[1,2,128,512]{2,3,1,0:T(8,128)(2,1)} %get-tuple-element.53) | copy-start | bytes 786436
  1085.8 12.3 %copy-start.10 = (bf16[1,2,128,512]{2,3,1,0:T(8,128)(2,1)S(1)}, bf16[1,2,128,512]{2,3,1,0:T(8,128)(2,1)}, u32[]{:S(2)}) copy-start(bf16[1,2,128,512]{2,3,1,0:T(8,128)(2,1)} %get-tuple-element.58) | copy-start | bytes 786436
  1085.8 14.9 %copy-start.6 = (bf16[1,1024,128]{1,2,0:T(8,128)(2,1)S(1)}, bf16[1,1024,128]{1,2,0:T(8,128)(2,1)}, u32[]{:S(2)}) copy-start(bf16[1,1024,128]{1,2,0:T(8,128)(2,1)} %copy-done.5) | copy-start | bytes 786436
  1085.8 14.9 %copy-start.8 = (bf16[1,1024,128]{1,2,0:T(8,128)(2,1)S(1)}, bf16[1,1024,128]{1,2,0:T(8,128)(2,1)}, u32[]{:S(2)}) copy-start(bf16[1,1024,128]{1,2,0:T(8,128)(2,1)} %copy-done.7) | copy-start | bytes 786436
Sparse Core Ops, SparseCore 0:
  144.4 13.7 reduce-scatter.12
  187.8 27.9 all-gather.6
  218.0 50.7 all-gather.4
  637.1 43.8 reduce-scatter.8
  695.4 13.8 reduce-scatter.14
  737.3 8.5 reduce-scatter.10
  764.5 29.1 all-gather.10
  795.8 50.7 all-gather.8
where the time goes:
time: 1190 us; the launch traced here: 1170 us
  local copies, waits for them, and re-layouts  592 us (50%)
  matrix products  190 us (16%)
  waiting for transfers between devices  169 us (14%)
  other arithmetic  127 us (11%)
  blocking collectives  70.2 us (6%)
  between operations  14.8 us (1%)
    add x2, local copies, waits for them, and re-layouts, on_device(): summed + tile_bias[:, :, None, :, None]  311 us
    reshape x2, local copies, waits for them, and re-layouts, on_device(): tile_sums = grad_pre.astype(jnp.float32).reshape(own_chan, tile_rows, TIL...  165 us
    all_to_all x1, waiting for transfers between devices, on_device(): lax.all_to_all(row_spec, 'gx', split_axis=2, concat_axis=3, tiled=True)  88 us
    unnamed x49, local copies, waits for them, and re-layouts  86.4 us
    reduce_sum x1, other arithmetic, on_device(): tile_sums = grad_pre.astype(jnp.float32).reshape(own_chan, tile_rows, TIL...  80.2 us
    dot_general x1, matrix products, on_device(): jnp.einsum('oi,ixy->oxy', w_rows, state_all, preferred_element_type=jnp.f...  60.1 us
    reduce_scatter x1, waiting for transfers between devices, on_device(): lax.psum_scatter(row_terms, 'gx', scatter_dimension=2, tiled=True)  44 us
    psum x1, blocking collectives, on_device(): point_grad, bias_grad = lax.psum((point_grad, bias_grad), ('gx', 'gy'))  37.7 us
  transfers between devices with their start and end apart: 9, of which 5 were waited for; matrix products, arithmetic and copies ran while one was open for 57% of the time, Pallas kernels for 0%

commit v1 on v0

v1 whole, which is shorter than its diff:
```python
import functools
import math

import jax
import jax.numpy as jnp
import numpy as np
from jax import lax
from jax.experimental import pallas as pl
from jax.experimental.pallas import tpu as pltpu
from jax.sharding import PartitionSpec as P

NX = 2048
NY = 2048
MX = 128
MY = 128
TILE = 16
NCLASS = 8

SCALE_FWD = 1.0 / math.sqrt(NX * NY)
SCALE_INV = 1.0 / math.sqrt(2.0 * MX * MY)
root_half = 0.7071067811865476
inv_root_tau = 0.3989422804014327

NN = (((1,), (0,)), ((), ()))
NT = (((1,), (1,)), ((), ()))
VMEM_LIMIT = 50 * 1024 * 1024


def host_tables():
    freq_y = np.arange(MY)
    angles = (freq_y[:, None] * np.arange(NY)[None, :] % NY).astype(np.float32)
    angles = angles * np.float32(2.0 * math.pi / NY)
    y_table = np.concatenate([np.cos(angles), -np.sin(angles)]).astype(jnp.bfloat16)
    freq_x = np.arange(MX)
    signed = np.where(freq_x < MX // 2, freq_x, freq_x - MX)
    angles = (np.arange(NX)[:, None] * signed[None, :] % NX).astype(np.float32)
    angles = angles * np.float32(2.0 * math.pi / NX)
    x_table = np.concatenate([np.cos(angles), np.sin(angles)], axis=1).astype(jnp.bfloat16)
    return y_table, x_table


def dot(a, b, dims=NN):
    return lax.dot_general(a, b, dims, preferred_element_type=jnp.float32)


def fwd_kernel(state_ref, y_ref, x_ref, out_ref):
    rows_t = dot(y_ref[...], state_ref[0], NT).astype(jnp.bfloat16)
    full = dot(rows_t, x_ref[...])
    out_ref[0, 0] = (full[:MY, :MX] + full[MY:, MX:]).astype(jnp.bfloat16)
    out_ref[1, 0] = (full[MY:, :MX] - full[:MY, MX:]).astype(jnp.bfloat16)


def expand_modes(modes_ref, x_ref, rows_scr, scale):
    cos, sin = x_ref[:, :MX], x_ref[:, MX:]
    left = (jnp.concatenate([cos, -sin], 1), jnp.concatenate([sin, cos], 1))

    def pair(p, carry):
        both = jnp.concatenate(
            [modes_ref[t, pl.ds(2 * p, 2)].reshape(2 * MY, MX) for t in range(2)], 1
        )
        for t in range(2):
            res = dot(left[t], both, NT) * scale
            for s in range(2):
                rows_scr[2 * p + s, :, t * MY:(t + 1) * MY] = res[
                    :, s * MY:(s + 1) * MY
                ].astype(jnp.bfloat16)
        return carry

    lax.fori_loop(0, rows_scr.shape[0] // 2, pair, 0)


def lane_weight():
    lane = lax.broadcasted_iota(jnp.int32, (1, 2 * MY), 1)
    return jnp.where(lane % MY == 0, SCALE_INV, 2.0 * SCALE_INV).astype(jnp.float32)


def gelu_parts(v):
    cdf = 0.5 + 0.5 * lax.erf(v * root_half)
    bell = jnp.exp(v * v * -0.5)
    return v * cdf, cdf + v * bell * inv_root_tau


def mid_kernel(state_ref, gout_ref, modes_ref, kron_ref, y_ref, x_ref, xt_ref, bias_ref,
               hot_ref, act_ref, gpre_ref, terms_ref, rows_scr, g_scr):
    step = pl.program_id(0)
    chans = gout_ref.shape[0]
    cols = gout_ref.shape[2]
    chunk = min(256, cols)

    @pl.when(step == 0)
    def _():
        expand_modes(modes_ref, x_ref, rows_scr, lane_weight())

    here = pl.ds(pl.multiple_of(step * TILE, TILE), TILE)
    rows = rows_scr[:, here, :].reshape(chans * TILE, 2 * MY)
    total = None
    for j in range(cols // chunk):
        lanes = slice(j * chunk, (j + 1) * chunk)
        cells = state_ref[:, :, lanes].reshape(-1, chunk)
        table = y_ref[:, lanes]
        pre = dot(kron_ref[...], cells) + dot(rows, table)
        bias = dot(bias_ref[...], hot_ref[0, :, lanes])
        parts = []
        for o in range(chans):
            v = pre[o * TILE:(o + 1) * TILE] + bias[o:o + 1]
            act, slope = gelu_parts(v)
            act_ref[o, :, lanes] = act.astype(jnp.bfloat16)
            grad = (gout_ref[o, :, lanes].astype(jnp.float32) * slope).astype(jnp.bfloat16)
            gpre_ref[o, :, lanes] = grad
            parts.append(grad)
        term = dot(jnp.concatenate(parts, 0), table, NT)
        total = term if total is None else total + term
    g_scr[:, here, :] = (total * lane_weight()).astype(jnp.bfloat16).reshape(chans, TILE, 2 * MY)

    @pl.when(step == pl.num_programs(0) - 1)
    def _():
        def one(o, carry):
            full = dot(xt_ref[...], g_scr[o])
            real = full[:MX, :MY] + full[MX:, MY:]
            imag = full[:MX, MY:] - full[MX:, :MY]
            terms_ref[0, o] = real.T.astype(jnp.bfloat16)
            terms_ref[1, o] = imag.T.astype(jnp.bfloat16)
            return carry

        lax.fori_loop(0, chans, one, 0)


def sums_kernel(state_ref, gpre_ref, hot_ref, point_ref, bias_ref, acc, acc_b):
    step = pl.program_id(0)
    chans, tile, cols = gpre_ref.shape
    every = state_ref.shape[0]

    @pl.when(step == 0)
    def _():
        acc[...] = jnp.zeros_like(acc)
        acc_b[...] = jnp.zeros_like(acc_b)

    grad = gpre_ref[...]
    acc[...] += dot(grad.reshape(chans * tile, cols), state_ref[...].reshape(every * tile, cols), NT)
    col = grad.astype(jnp.float32).sum(axis=1)
    high = col.astype(jnp.bfloat16)
    low = (col - high.astype(jnp.float32)).astype(jnp.bfloat16)
    acc_b[...] += dot(high, hot_ref[0], NT) + dot(low, hot_ref[0], NT)

    @pl.when(step == pl.num_programs(0) - 1)
    def _():
        shape = (chans * tile, every * tile)
        row = lax.broadcasted_iota(jnp.int32, shape, 0) % tile
        lane = lax.broadcasted_iota(jnp.int32, shape, 1) % tile
        kept = jnp.where(row == lane, acc[...], 0.0)
        group = lax.broadcasted_iota(jnp.int32, (every * tile, every), 0) // tile
        which = lax.broadcasted_iota(jnp.int32, (every * tile, every), 1)
        ones = (group == which).astype(jnp.float32)
        summed = lax.dot_general(kept, ones, NN, precision=lax.Precision.HIGHEST,
                                 preferred_element_type=jnp.float32)
        point_ref[...] = summed.reshape(chans, tile, every).sum(axis=1) * SCALE_FWD
        bias_ref[...] = acc_b[...] * SCALE_FWD


def back_kernel(grad_ref, modes_ref, kron_ref, y_ref, x_ref, out_ref, rows_scr):
    step = pl.program_id(0)
    chans, tile, cols = out_ref.shape
    chunk = min(256, cols)

    @pl.when(step == 0)
    def _():
        expand_modes(modes_ref, x_ref, rows_scr, SCALE_FWD)

    here = pl.ds(pl.multiple_of(step * TILE, TILE), TILE)
    rows = rows_scr[:, here, :].reshape(chans * TILE, 2 * MY)
    for j in range(cols // chunk):
        lanes = slice(j * chunk, (j + 1) * chunk)
        cells = grad_ref[:, :, lanes].reshape(-1, chunk)
        res = dot(kron_ref[...], cells) + dot(rows, y_ref[:, lanes])
        out_ref[:, :, lanes] = res.astype(jnp.bfloat16).reshape(chans, tile, chunk)


def whole(array):
    return pl.BlockSpec(array.shape, lambda *_: (0,) * array.ndim)


def call(kernel, name, grid, in_specs, out_specs, out_shape, scratch, cost):
    return pl.pallas_call(
        kernel, grid=grid, in_specs=in_specs, out_specs=out_specs, out_shape=out_shape,
        scratch_shapes=scratch, name=name,
        compiler_params=pltpu.CompilerParams(
            dimension_semantics=("arbitrary",), vmem_limit_bytes=VMEM_LIMIT
        ),
        cost_estimate=pl.CostEstimate(flops=cost[0], bytes_accessed=cost[1], transcendentals=0),
    )


def mix_modes(weight, spectrum):
    real_part = jnp.einsum("iokm,ikm->okm", weight[0], spectrum[0], precision="highest") - jnp.einsum(
        "iokm,ikm->okm", weight[1], spectrum[1], precision="highest"
    )
    imag_part = jnp.einsum("iokm,ikm->okm", weight[0], spectrum[1], precision="highest") + jnp.einsum(
        "iokm,ikm->okm", weight[1], spectrum[0], precision="highest"
    )
    return jnp.stack([real_part, imag_part])


def back_mix(weight, grad_modes):
    real_part = jnp.einsum("iokm,okm->ikm", weight[0], grad_modes[0], precision="highest") + jnp.einsum(
        "iokm,okm->ikm", weight[1], grad_modes[1], precision="highest"
    )
    imag_part = jnp.einsum("iokm,okm->ikm", weight[0], grad_modes[1], precision="highest") - jnp.einsum(
        "iokm,okm->ikm", weight[1], grad_modes[0], precision="highest"
    )
    return jnp.stack([real_part, imag_part])


def weight_grad(spectrum, grad_modes):
    s = spectrum[:, :, None]
    g = grad_modes[:, None]
    return jnp.stack([s[0] * g[0] + s[1] * g[1], s[0] * g[1] - s[1] * g[0]])


def scatter_sum(terms, n_gx, n_gy):
    two, chans = terms.shape[:2]
    own_k, own_m = MY // n_gx, MX // n_gy
    blocks = terms.reshape(two, chans, n_gx, own_k, n_gy, own_m).transpose(2, 4, 0, 1, 3, 5)
    blocks = blocks.reshape(n_gx * n_gy, two, chans, own_k, own_m)
    got = lax.all_to_all(blocks, ("gx", "gy"), split_axis=0, concat_axis=0, tiled=True)
    return got.astype(jnp.float32).sum(axis=0)


def gather_modes(modes):
    along = lax.all_gather(modes, "gy", axis=3, tiled=True)
    return lax.all_gather(along, "gx", axis=2, tiled=True)


def on_device(n_gx, n_gy, state_in, tile_class, class_bias, w_point, spec_weight, grad_out):
    chans, rows, cols = state_in.shape
    every = w_point.shape[0]
    gx_index = lax.axis_index("gx")
    gy_index = lax.axis_index("gy")
    col_index = lax.axis_index("col")
    bf16 = jnp.bfloat16
    y_all, x_all = host_tables()
    y_table = lax.dynamic_slice_in_dim(jnp.asarray(y_all), gy_index * cols, cols, 1)
    x_table = lax.dynamic_slice_in_dim(jnp.asarray(x_all), gx_index * rows, rows, 0)
    x_table_t = lax.dynamic_slice_in_dim(jnp.asarray(x_all.T.copy()), gx_index * rows, rows, 1)
    state_all = lax.all_gather(state_in, "col", axis=0, tiled=True)
    w_rows = lax.dynamic_slice_in_dim(w_point, col_index * chans, chans, 0)
    w_cols = lax.dynamic_slice_in_dim(w_point, col_index * chans, chans, 1)
    same = jnp.eye(TILE, dtype=bf16)
    kron_fwd = (w_rows[:, None, :, None] * same[None, :, None, :]).reshape(chans * TILE, every * TILE)
    kron_bwd = (w_cols.T[:, None, :, None] * same[None, :, None, :]).reshape(
        chans * TILE, every * TILE
    )
    hot = (
        jnp.repeat(tile_class, TILE, axis=1)[:, None, :]
        == (jnp.arange(2 * NCLASS, dtype=jnp.int32) % NCLASS)[None, :, None]
    ).astype(bf16)
    bias_own = lax.dynamic_slice_in_dim(class_bias, col_index * chans, chans, 1).T
    bias_high = bias_own.astype(bf16)
    bias_low = (bias_own - bias_high.astype(jnp.float32)).astype(bf16)
    bias_pair = jnp.concatenate([bias_high, bias_low], 1)

    steps = rows // TILE
    cells = rows * cols
    wide = 2 * MY
    block = pl.BlockSpec((chans, TILE, cols), lambda b: (0, b, 0))
    block_all = pl.BlockSpec((every, TILE, cols), lambda b: (0, b, 0))
    block_hot = pl.BlockSpec((1, 2 * NCLASS, cols), lambda b: (b, 0, 0))
    modes_shape = jax.ShapeDtypeStruct((2, chans, MY, MX), bf16)
    field_shape = jax.ShapeDtypeStruct((chans, rows, cols), bf16)
    rows_scratch = pltpu.VMEM((chans, rows, wide), bf16)

    terms = call(
        fwd_kernel, "forward_transform", (chans,),
        [pl.BlockSpec((1, rows, cols), lambda c: (c, 0, 0)), whole(y_table), whole(x_table)],
        pl.BlockSpec((2, 1, MY, MX), lambda c: (0, c, 0, 0)),
        modes_shape, [], (2 * chans * cells * wide, 2 * chans * cells),
    )(state_in, y_table, x_table)
    spectrum = scatter_sum(terms, n_gx, n_gy) * SCALE_FWD
    spec_all = lax.all_gather(spectrum, "col", axis=1, tiled=True)
    weight_f = spec_weight.astype(jnp.float32)
    mixed = mix_modes(weight_f, spec_all).astype(bf16)
    mixed_all = gather_modes(mixed)

    act_out, grad_pre, grad_terms = call(
        mid_kernel, "layer_and_adjoint", (steps,),
        [block_all, block, whole(modes_shape), whole(kron_fwd), whole(y_table), whole(x_table),
         whole(x_table_t), whole(bias_pair), block_hot],
        [block, block, whole(modes_shape)],
        [field_shape, field_shape, modes_shape],
        [rows_scratch, rows_scratch],
        (2 * chans * cells * (2 * wide + every * TILE), 10 * chans * cells),
    )(state_all, grad_out, mixed_all, kron_fwd, y_table, x_table, x_table_t, bias_pair, hot)

    grad_all = lax.all_gather(grad_pre, "col", axis=0, tiled=True)
    point_sum, bias_sum = call(
        sums_kernel, "weight_sums", (steps,), [block_all, block, block_hot],
        [pl.BlockSpec((chans, every), lambda b: (0, 0)),
         pl.BlockSpec((chans, 2 * NCLASS), lambda b: (0, 0))],
        [jax.ShapeDtypeStruct((chans, every), jnp.float32),
         jax.ShapeDtypeStruct((chans, 2 * NCLASS), jnp.float32)],
        [pltpu.VMEM((chans * TILE, every * TILE), jnp.float32),
         pltpu.VMEM((chans, 2 * NCLASS), jnp.float32)],
        (2 * chans * cells * every * TILE, 6 * chans * cells),
    )(state_all, grad_pre, hot)
    sums = jnp.concatenate([point_sum, bias_sum], 1)
    sums = lax.all_gather(sums, ("gx", "gy"), axis=0, tiled=False).sum(axis=0)
    point_grad = sums[:, :every]
    bias_grad = sums[:, every:every + NCLASS].T

    grad_modes = scatter_sum(grad_terms, n_gx, n_gy)
    input_terms = back_mix(weight_f, grad_modes)
    input_modes = lax.psum_scatter(input_terms, "col", scatter_dimension=1, tiled=True).astype(bf16)
    input_all = gather_modes(input_modes)
    spec_grad = weight_grad(spec_all, grad_modes)

    grad_in = call(
        back_kernel, "input_gradient", (steps,),
        [block_all, whole(modes_shape), whole(kron_bwd), whole(y_table), whole(x_table)],
        block, field_shape, [rows_scratch],
        (2 * chans * cells * (wide + every * TILE), 6 * chans * cells),
    )(grad_all, input_all, kron_bwd, y_table, x_table)
    return (act_out, grad_in, spec_grad, point_grad, bias_grad)


def solution(mesh):
    return jax.shard_map(
        functools.partial(on_device, mesh.shape["gx"], mesh.shape["gy"]),
        mesh=mesh,
        in_specs=(
            P(("groups", "col"), "gx", "gy"),
            P(("groups", "gx"), "gy"),
            P(),
            P(),
            P(None, None, "col", "gx", "gy"),
            P(("groups", "col"), "gx", "gy"),
        ),
        out_specs=(
            P(("groups", "col"), "gx", "gy"),
            P(("groups", "col"), "gx", "gy"),
            P("groups", None, "col", "gx", "gy"),
            P(("groups", "col"), None),
            P("groups", "col"),
        ),
        check_vma=False,
    )
```

time: 1190 us -> 452 us (0.38); the launches traced: 1170 us -> 448 us
  local copies, waits for them, and re-layouts: 592 us -> 44.2 us
  matrix products: 190 us -> 0 us
  Pallas kernels: 0 us -> 148 us
  other arithmetic: 127 us -> 34.7 us
  waiting for transfers between devices: 169 us -> 78.3 us
  blocking collectives: 70.2 us -> 128 us
    add x2 -> x0, local copies, waits for them, and re-layouts: 311 us -> none  [on_device(): summed + tile_bias[:, :, None, :, None]]
    dot_general x12 -> x0, matrix products: 190 us -> none  [the longest x1 60.1 us: on_device(): jnp.einsum('oi,ixy->oxy', w_rows, state_all, preferred_element_type=jnp.f...]
    reshape x2 -> x4, local copies, waits for them, and re-layouts: 165 us -> 7.62 us  [scatter_sum(): terms.reshape(two, chans, n_gx, own_k, n_gy, own_m)]
    pallas_call x0 -> x4, Pallas kernels: none -> 148 us  [the longest x1 60.4 us: on_device(): call(mid_kernel, 'layer_and_adjoint', (steps,), [block_all, block, whole(...]
    all_to_all x1 -> x0, waiting for transfers between devices: 88 us -> none  [on_device(): lax.all_to_all(row_spec, 'gx', split_axis=2, concat_axis=3, tiled=True)]
    reduce_sum x1 -> x3, other arithmetic: 80.2 us -> 0.85 us  [the longest x2 0.84 us: scatter_sum(): return got.astype(jnp.float32).sum(axis=0)]
    unnamed x49 -> x30, local copies, waits for them, and re-layouts: 86.4 us -> 17.3 us
    all_to_all x0 -> x2, blocking collectives: none -> 65.2 us  [scatter_sum(): lax.all_to_all(blocks, ('gx', 'gy'), split_axis=0, concat_axis=0, tiled=T...]
  transfers between devices with their start and end apart: 9 -> 5, of which waited for: 5 -> 3; matrix products, arithmetic and copies ran while one was open for 57% -> 7% of each run, Pallas kernels for 0% -> 8%
where the time goes in v1:
time: 452 us; the launch traced here: 448 us
  Pallas kernels  148 us (33%)
  blocking collectives  128 us (28%)
  waiting for transfers between devices  78.3 us (17%)
  local copies, waits for them, and re-layouts  44.2 us (10%)
  other arithmetic  34.7 us (8%)
  between operations  14.1 us (3%)
    all_to_all x2, blocking collectives, scatter_sum(): lax.all_to_all(blocks, ('gx', 'gy'), split_axis=0, concat_axis=0, tiled=T...  65.2 us
    pallas_call x1, Pallas kernels, on_device(): call(mid_kernel, 'layer_and_adjoint', (steps,), [block_all, block, whole(...  60.4 us
    all_gather x1, waiting for transfers between devices, on_device(): state_all = lax.all_gather(state_in, 'col', axis=0, tiled=True)  52.3 us
    pallas_call x1, Pallas kernels, on_device(): call(back_kernel, 'input_gradient', (steps,), [block_all, whole(modes_sha...  37.3 us
    pallas_call x1, Pallas kernels, on_device(): call(sums_kernel, 'weight_sums', (steps,), [block_all, block, block_hot],...  33.9 us
    all_gather x1, blocking collectives, on_device(): sums = lax.all_gather(sums, ('gx', 'gy'), axis=0, tiled=False).sum(axis=0)  30.8 us
    all_gather x2, blocking collectives, gather_modes(): along = lax.all_gather(modes, 'gy', axis=3, tiled=True)  29.4 us
    all_gather x2, waiting for transfers between devices, gather_modes(): return lax.all_gather(along, 'gx', axis=2, tiled=True)  17.9 us
  transfers between devices with their start and end apart: 5, of which 3 were waited for; matrix products, arithmetic and copies ran while one was open for 7% of the time, Pallas kernels for 8%

profile of v1, /device:TPU:0, one launch (start us, length us, event | category | flops | bytes accessed | tf_op | source)
XLA Modules:
  0.0 448.2 jit_solution(12460549472339577092)
XLA Ops:
  7.2 1.0 constant_dynamic-slice_fusion.3.x_ref
  8.2 1.1 constant_dynamic-slice_fusion.4.y_ref
  9.3 16.5 %forward_transform.1 = bf16[2,16,128,128]{3,2,1,0:T(8,128)(2,1)S(1)} custom-call(bf16[16,512,1024]{2,1,0:T(8,128)(2,1)} %state_ref.1, bf16[256,1024]{1,0:T(8,128)(2,1)S(1)} %constant_dynamic-slice_fusion.4.y_ref, bf16[512,256]{1,0:T(8,128)(2,1)S(1)} %constant_dynamic-slice_fusion.3.x_ref), custom_call_target="tpu_custom_call" | custom-call | flops 4294967296 | bytes 16777216 | tf_op jit(solution)/shard_map/forward_transform/pallas_call | solution.py:271
  25.8 1.8 reshape.78
  27.7 2.0 copy.24
  29.7 2.7 reshape.101
  32.3 33.1 %all_to_all.10 = bf16[8,2,32768]{2,1,0:T(2,128)(2,1)} all-to-all(bf16[8,2,32768]{2,1,0:T(2,128)(2,1)} %reshape.101), channel_id=1, replica_groups=mesh['groups'=2,'gx'=4,'gy'=2,'col'=2] {'gx','gy'}, dimensions={0} | all-to-all | bytes 2097152 | tf_op jit(solution)/shard_map/all_to_all | solution.py:224
  65.5 3.1 reshape.102
  68.6 0.4 convert_reduce_fusion.1
  69.0 2.6 all_gather.28
  71.6 1.3 slice_bitcast_fusion.3
  72.9 6.3 %fusion.2 = (f32[32,64,16]{1,0,2:T(8,128)S(1)}, f32[32,64,16]{1,0,2:T(8,128)S(1)}, f32[32,64,16]{1,0,2:T(8,128)S(1)}, f32[32,64,16]{1,0,2:T(8,128)S(1)}) fusion(f32[32,64,32]{1,0,2:T(8,128)S(1)} %get-tuple-element.48, bf16[2,32,16,32,64]{4,3,2,1,0:T(8,128)(2,1)} %param.13, f32[32,64,32]{1,0,2:T(8,128)S(1)} %get-tuple-element.47), kind=kLoop, calls=%fused_computation.11 | loop fusion | flops 10354688 | bytes 5242880
  79.2 0.3 copy.49
  79.4 0.3 copy.57
  80.6 14.6 %all_gather.29 = bf16[2,16,32,128]{2,1,0,3:T(8,128)(2,1)S(1)} all-gather(bf16[2,16,32,64]{2,1,0,3:T(8,128)(2,1)S(1)} %pad_maximum_fusion.2), channel_id=1, replica_groups=mesh['groups'=2,'gx'=4,'gy'=2,'col'=2] {'gy'}, dimensions={3}, use_global_device_ids=true | all-gather | bytes 393216 | tf_op jit(solution)/shard_map/all_gather | solution.py:229
  95.2 1.8 copy.25
  97.1 0.7 all-gather.6.cloned.1.call-update
  98.7 1.7 broadcast_multiply_fusion
  100.4 3.6 mul.132.kron_ref
  104.1 1.0 constant_dynamic-slice_fusion.1.xt_ref
  105.0 1.3 compare_convert_fusion.hot_ref
  106.3 17.9 %all-gather.8.cloned.1.call-done.modes_ref = bf16[2,16,128,128]{3,2,1,0:T(8,128)(2,1)} async-done(((bf16[2,16,32,128]{3,2,1,0:T(8,128)(2,1)}), bf16[2,16,128,128]{3,2,1,0:T(8,128)(2,1)}) %all-gather.8.cloned.1.call-update) | async-done | bytes 1048592 | tf_op jit(solution)/shard_map/all_gather | solution.py:230
  124.2 52.3 %all-gather.6.cloned.1.call-done.state_ref = bf16[32,512,1024]{2,1,0:T(8,128)(2,1)} async-done(((bf16[16,512,1024]{2,1,0:T(8,128)(2,1)}), bf16[32,512,1024]{2,1,0:T(8,128)(2,1)}) %all-gather.6.cloned.1.call-update) | async-done | bytes 33554448 | tf_op jit(solution)/shard_map/all_gather | solution.py:244
  176.5 1.2 copy-done.4
  177.7 60.4 %layer_and_adjoint.1 = (bf16[16,512,1024]{2,1,0:T(8,128)(2,1)}, bf16[16,512,1024]{2,1,0:T(8,128)(2,1)}, bf16[2,16,128,128]{3,2,1,0:T(8,128)(2,1)S(1)}) custom-call(bf16[32,512,1024]{2,1,0:T(8,128)(2,1)} %all-gather.6.cloned.1.call-done.state_ref, bf16[16,512,1024]{2,1,0:T(8,128)(2,1)} %gout_ref.1, bf16[2,16,128,128]{3,2,1,0:T(8,128)(2,1)S(1)} %copy-done.4, ...), custom_call_target="tpu_custom_call" | custom-call | flops 17179869184 | bytes 83886080 | tf_op jit(solution)/shard_map/layer_and_adjoint/pallas_call | solution.py:283
  238.1 1.8 reshape.80
  240.0 2.0 copy.29
  241.9 2.7 reshape.103
  244.6 32.1 %all_to_all.11 = bf16[8,2,32768]{2,1,0:T(2,128)(2,1)} all-to-all(bf16[8,2,32768]{2,1,0:T(2,128)(2,1)} %reshape.103), channel_id=1, replica_groups=mesh['groups'=2,'gx'=4,'gy'=2,'col'=2] {'gx','gy'}, dimensions={0} | all-to-all | bytes 2097152 | tf_op jit(solution)/shard_map/all_to_all | solution.py:224
  276.7 3.1 reshape.104
  279.8 0.4 convert_reduce_fusion
  280.2 0.8 slice_bitcast_fusion.7
  281.1 7.8 %fusion.6 = (f32[32,64,32]{1,0,2:T(8,128)S(1)}, f32[32,64,32]{1,0,2:T(8,128)S(1)}, f32[32,64,32]{1,0,2:T(8,128)S(1)}, f32[32,64,32]{1,0,2:T(8,128)S(1)}) fusion(f32[32,64,16]{1,0,2:T(8,128)S(1)} %get-tuple-element.52, bf16[2,32,16,32,64]{4,3,2,1,0:T(8,128)(2,1)} %param.13, f32[32,64,16]{1,0,2:T(8,128)S(1)} %get-tuple-element.51), kind=kLoop, calls=%fused_computation.15 | loop fusion | flops 10223616 | bytes 5505024 | tf_op jit(solution)/shard_map/iokm,okm->ikm/dot_general | solution.py:204
  289.2 1.2 reshape.99
  290.4 7.1 %reduce-scatter.4.cloned.1.call-done = f32[16,4096]{1,0:T(8,128)} async-done(((f32[32,4096]{1,0:T(8,128)}), f32[16,4096]{1,0:T(8,128)}) %reduce-scatter.4.cloned.1.call-update) | async-done | bytes 262160
  297.5 1.2 reshape.100
  298.8 0.8 copy.30
  299.5 14.8 %all_gather.32 = bf16[2,16,32,128]{2,1,0,3:T(8,128)(2,1)S(1)} all-gather(bf16[2,16,32,64]{2,1,0,3:T(8,128)(2,1)S(1)} %copy.30), channel_id=1, replica_groups=mesh['groups'=2,'gx'=4,'gy'=2,'col'=2] {'gy'}, dimensions={3}, use_global_device_ids=true | all-gather | bytes 393216 | tf_op jit(solution)/shard_map/all_gather | solution.py:229
  314.3 1.8 copy.31
  316.4 0.3 all-gather.10.cloned.1.call-update
  316.7 4.5 %mul.135.kron_ref = bf16[256,512]{1,0:T(8,128)(2,1)S(1)} reshape(bf16[16,16,32,16]{3,2,1,0:T(8,128)(2,1)} %get-tuple-element.54) | data formatting | bytes 524288 | tf_op jit(solution)/shard_map/mul | solution.py:249
  321.3 33.9 %weight_sums.1 = (f32[16,32]{1,0:T(8,128)S(1)}, f32[16,16]{1,0:T(8,128)S(1)}) custom-call(bf16[32,512,1024]{2,1,0:T(8,128)(2,1)} %all-gather.6.cloned.1.call-done.state_ref, bf16[16,512,1024]{2,1,0:T(8,128)(2,1)} %get-tuple-element.11.gpre_ref, bf16[32,16,1024]{2,1,0:T(8,128)(2,1)S(1)} %copy-done.2), custom_call_target="tpu_custom_call" | custom-call | flops 8589934592 | bytes 50331648 | tf_op jit(solution)/shard_map/weight_sums/pallas_call | solution.py:294
  355.3 30.8 %all-gather = f32[128,48]{1,0:T(8,128)S(1)} all-gather(f32[16,48]{1,0:T(8,128)S(1)} %pad_maximum_fusion.3), channel_id=2, replica_groups=mesh['groups'=2,'gx'=4,'gy'=2,'col'=2] {'gx','gy'}, dimensions={0}, use_global_device_ids=true | all-gather | bytes 27648 | tf_op jit(solution)/shard_map/all_gather | solution.py:305
  386.3 0.7 copy.33
  386.9 6.1 %multiply_add_fusion = (f32[1,32,16,32,64]{4,3,2,1,0:T(8,128)S(1)}, f32[1,32,16,32,64]{4,3,2,1,0:T(8,128)}) fusion(f32[16,32,64]{2,1,0:T(8,128)} %get-tuple-element.53, f32[32,32,64]{2,1,0:T(8,128)S(1)} %copy-done.6, f32[16,32,64]{2,1,0:T(8,128)S(1)} %get-tuple-element.50, f32[32,32,64]{2,1,0:T(8,128)S(1)} %copy-done.5), kind=kLoop, calls=%fused_computation.18 | loop fusion | flops 6291456 | bytes 9175040 | tf_op jit(solution)/shard_map/add | solution.py:216
  393.0 10.1 %pad_maximum_fusion = f32[2,32,16,32,64]{4,3,2,1,0:T(8,128)} fusion(f32[1,32,16,32,64]{4,3,2,1,0:T(8,128)} %get-tuple-element.45, f32[1,32,16,32,64]{4,3,2,1,0:T(8,128)S(1)} %get-tuple-element.44), kind=kLoop, calls=%fused_computation | loop fusion | flops 2097152 | bytes 16777216 | tf_op jit(solution)/shard_map/stack | solution.py:216
  403.1 1.2 copy-done.3
  404.3 37.3 %input_gradient.1 = bf16[16,512,1024]{2,1,0:T(8,128)(2,1)} custom-call(bf16[32,512,1024]{2,1,0:T(8,128)(2,1)} %all-gather.10.cloned.1.call-done.grad_ref, bf16[2,16,128,128]{3,2,1,0:T(8,128)(2,1)S(1)} %copy-done.3, bf16[256,512]{1,0:T(8,128)(2,1)S(1)} %mul.135.kron_ref, bf16[256,1024]{1,0:T(8,128)(2,1)S(1)} %constant_dynamic-slice_fusion.4.y_ref, ...), custom_call_target="tpu_custom_call" | custom-call | flops 12884901888 | bytes 50331648 | tf_op jit(solution)/shard_map/input_gradient/pallas_call | solution.py:315
  (52 shorter events, 2.7 us)
Async XLA Ops:
  7.2 91.0 %copy-start = (bf16[32,32]{1,0:T(8,128)(2,1)S(1)}, bf16[32,32]{1,0:T(8,128)(2,1)}, u32[]{:S(2)}) copy-start(bf16[32,32]{1,0:T(8,128)(2,1)} %param.12) | copy-start | bytes 6148
  7.2 117.0 %all-gather.8.cloned.1.call-start = ((), (), s32[]{:S(2)}) async-start(), calls=%async_computation.4 | async-start | bytes 1310720 | tf_op jit(solution)/shard_map/all_gather | solution.py:230
  97.0 1.0 copy-start.9
  97.1 1.3 copy-start.8
  97.1 79.4 %all-gather.6.cloned.1.call-start = ((), (), s32[]{:S(2)}) async-start(), calls=%async_computation.3 | async-start | bytes 50331648 | tf_op jit(solution)/shard_map/all_gather | solution.py:244
  97.8 199.7 %reduce-scatter.4.cloned.1.call-start = ((), (), s32[]{:S(2)}) async-start(), calls=%async_computation.7 | async-start | bytes 786432
  176.5 1.2 copy-start.4
  290.4 112.8 %all-gather.12.cloned.1.call-start = ((), (), s32[]{:S(2)}) async-start(), calls=%async_computation.6 | async-start | bytes 1310720 | tf_op jit(solution)/shard_map/all_gather | solution.py:230
  316.2 87.0 %all-gather.10.cloned.1.call-start = ((), (), s32[]{:S(2)}) async-start(), calls=%async_computation.5 | async-start | bytes 50331648 | tf_op jit(solution)/shard_map/all_gather | solution.py:293
  316.4 4.9 %copy-start.2 = (bf16[32,16,1024]{2,1,0:T(8,128)(2,1)S(1)}, bf16[32,16,1024]{2,1,0:T(8,128)(2,1)}, u32[]{:S(2)}) copy-start(bf16[32,16,1024]{2,1,0:T(8,128)(2,1)} %compare_convert_fusion.hot_ref) | copy-start | bytes 3145732
  321.3 65.6 %copy-start.5 = (f32[32,32,64]{2,1,0:T(8,128)S(1)}, f32[32,32,64]{2,1,0:T(8,128)}, u32[]{:S(2)}) copy-start(f32[32,32,64]{2,1,0:T(8,128)} %get-tuple-element.46) | copy-start | bytes 786436
  321.3 65.6 %copy-start.6 = (f32[32,32,64]{2,1,0:T(8,128)S(1)}, f32[32,32,64]{2,1,0:T(8,128)}, u32[]{:S(2)}) copy-start(f32[32,32,64]{2,1,0:T(8,128)} %get-tuple-element.49) | copy-start | bytes 786436
  386.2 6.8 %copy-start.7 = (f32[16,48]{1,0:T(8,128)}, f32[16,48]{1,0:T(8,128)S(1)}, u32[]{:S(2)}) copy-start(f32[16,48]{1,0:T(8,128)S(1)} %reduce_sum.29) | copy-start | bytes 9220
  403.1 1.2 copy-start.3
  404.3 37.3 %copy-start.1 = (bf16[32,32]{1,0:T(8,128)(2,1)S(1)}, bf16[32,32]{1,0:T(8,128)(2,1)}, u32[]{:S(2)}) copy-start(bf16[32,32]{1,0:T(8,128)(2,1)} %param.12) | copy-start | bytes 6148
Sparse Core Ops, SparseCore 0:
  97.2 26.9 all-gather.7
  125.7 50.7 all-gather.5
  290.5 6.9 reduce-scatter.3
  316.3 29.0 all-gather.11
  347.4 50.7 all-gather.9

commit v2 on v1

--- a/solution.py
+++ b/solution.py
@@ -26,7 +26,7 @@
 VMEM_LIMIT = 50 * 1024 * 1024
 
 
-def host_tables():
+def host_tables(n_gy):
     freq_y = np.arange(MY)
     angles = (freq_y[:, None] * np.arange(NY)[None, :] % NY).astype(np.float32)
     angles = angles * np.float32(2.0 * math.pi / NY)
@@ -35,8 +35,9 @@
     signed = np.where(freq_x < MX // 2, freq_x, freq_x - MX)
     angles = (np.arange(NX)[:, None] * signed[None, :] % NX).astype(np.float32)
     angles = angles * np.float32(2.0 * math.pi / NX)
-    x_table = np.concatenate([np.cos(angles), np.sin(angles)], axis=1).astype(jnp.bfloat16)
-    return y_table, x_table
+    cos, sin = (f(angles).reshape(NX, n_gy, 1, MX // n_gy) for f in (np.cos, np.sin))
+    x_table = np.stack([np.concatenate([cos, -sin], 2), np.concatenate([sin, cos], 2)])
+    return y_table, x_table.reshape(2, NX, 2 * MX).astype(jnp.bfloat16)
 
 
 def dot(a, b, dims=NN):
@@ -45,21 +46,25 @@
 
 def fwd_kernel(state_ref, y_ref, x_ref, out_ref):
     rows_t = dot(y_ref[...], state_ref[0], NT).astype(jnp.bfloat16)
-    full = dot(rows_t, x_ref[...])
-    out_ref[0, 0] = (full[:MY, :MX] + full[MY:, MX:]).astype(jnp.bfloat16)
-    out_ref[1, 0] = (full[MY:, :MX] - full[:MY, MX:]).astype(jnp.bfloat16)
+    full = dot(rows_t[:MY], x_ref[0]) + dot(rows_t[MY:], x_ref[1])
+    wide = out_ref.shape[-1]
+    for g in range(out_ref.shape[0]):
+        out_ref[g, 0] = full[:, g * wide:(g + 1) * wide].astype(jnp.bfloat16)
 
 
 def expand_modes(modes_ref, x_ref, rows_scr, scale):
-    cos, sin = x_ref[:, :MX], x_ref[:, MX:]
-    left = (jnp.concatenate([cos, -sin], 1), jnp.concatenate([sin, cos], 1))
+    n_gy, wide = modes_ref.shape[0], modes_ref.shape[3]
 
     def pair(p, carry):
-        both = jnp.concatenate(
-            [modes_ref[t, pl.ds(2 * p, 2)].reshape(2 * MY, MX) for t in range(2)], 1
-        )
+        parts = [modes_ref[g, pl.ds(2 * p, 2)].reshape(2 * MY, wide) for g in range(n_gy)]
         for t in range(2):
-            res = dot(left[t], both, NT) * scale
+            if wide % 128 == 0:
+                res = dot(x_ref[t], jnp.concatenate(parts, 1), NT)
+            else:
+                res = sum(
+                    dot(x_ref[t, :, g * wide:(g + 1) * wide], parts[g], NT) for g in range(n_gy)
+                )
+            res = res * scale
             for s in range(2):
                 rows_scr[2 * p + s, :, t * MY:(t + 1) * MY] = res[
                     :, s * MY:(s + 1) * MY
@@ -80,7 +85,7 @@
     return v * cdf, cdf + v * bell * inv_root_tau
 
 
-def mid_kernel(state_ref, gout_ref, modes_ref, kron_ref, y_ref, x_ref, xt_ref, bias_ref,
+def mid_kernel(state_ref, other_ref, gout_ref, modes_ref, kron_ref, y_ref, x_ref, xt_ref, bias_ref,
                hot_ref, act_ref, gpre_ref, terms_ref, rows_scr, g_scr):
     step = pl.program_id(0)
     chans = gout_ref.shape[0]
@@ -97,8 +102,9 @@
     for j in range(cols // chunk):
         lanes = slice(j * chunk, (j + 1) * chunk)
         cells = state_ref[:, :, lanes].reshape(-1, chunk)
+        others = other_ref[:, :, lanes].reshape(-1, chunk)
         table = y_ref[:, lanes]
-        pre = dot(kron_ref[...], cells) + dot(rows, table)
+        pre = dot(kron_ref[0], cells) + dot(kron_ref[1], others) + dot(rows, table)
         bias = dot(bias_ref[...], hot_ref[0, :, lanes])
         parts = []
         for o in range(chans):
@@ -115,20 +121,19 @@
     @pl.when(step == pl.num_programs(0) - 1)
     def _():
         def one(o, carry):
-            full = dot(xt_ref[...], g_scr[o])
-            real = full[:MX, :MY] + full[MX:, MY:]
-            imag = full[:MX, MY:] - full[MX:, :MY]
-            terms_ref[0, o] = real.T.astype(jnp.bfloat16)
-            terms_ref[1, o] = imag.T.astype(jnp.bfloat16)
+            full = (dot(xt_ref[0], g_scr[o, :, :MY]) + dot(xt_ref[1], g_scr[o, :, MY:])).T
+            wide = terms_ref.shape[-1]
+            for g in range(terms_ref.shape[0]):
+                terms_ref[g, o] = full[:, g * wide:(g + 1) * wide].astype(jnp.bfloat16)
             return carry
 
         lax.fori_loop(0, chans, one, 0)
 
 
-def sums_kernel(state_ref, gpre_ref, hot_ref, point_ref, bias_ref, acc, acc_b):
+def sums_kernel(state_ref, other_ref, gpre_ref, hot_ref, point_ref, bias_ref, acc, acc_b):
     step = pl.program_id(0)
     chans, tile, cols = gpre_ref.shape
-    every = state_ref.shape[0]
+    every = 2 * chans
 
     @pl.when(step == 0)
     def _():
@@ -136,7 +141,9 @@
         acc_b[...] = jnp.zeros_like(acc_b)
 
     grad = gpre_ref[...]
-    acc[...] += dot(grad.reshape(chans * tile, cols), state_ref[...].reshape(every * tile, cols), NT)
+    flat = grad.reshape(chans * tile, cols)
+    acc[:, :chans * tile] += dot(flat, state_ref[...].reshape(chans * tile, cols), NT)
+    acc[:, chans * tile:] += dot(flat, other_ref[...].reshape(chans * tile, cols), NT)
     col = grad.astype(jnp.float32).sum(axis=1)
     high = col.astype(jnp.bfloat16)
     low = (col - high.astype(jnp.float32)).astype(jnp.bfloat16)
@@ -157,7 +164,7 @@
         bias_ref[...] = acc_b[...] * SCALE_FWD
 
 
-def back_kernel(grad_ref, modes_ref, kron_ref, y_ref, x_ref, out_ref, rows_scr):
+def back_kernel(grad_ref, other_ref, modes_ref, kron_ref, y_ref, x_ref, out_ref, rows_scr):
     step = pl.program_id(0)
     chans, tile, cols = out_ref.shape
     chunk = min(256, cols)
@@ -171,7 +178,8 @@
     for j in range(cols // chunk):
         lanes = slice(j * chunk, (j + 1) * chunk)
         cells = grad_ref[:, :, lanes].reshape(-1, chunk)
-        res = dot(kron_ref[...], cells) + dot(rows, y_ref[:, lanes])
+        others = other_ref[:, :, lanes].reshape(-1, chunk)
+        res = dot(kron_ref[0], cells) + dot(kron_ref[1], others) + dot(rows, y_ref[:, lanes])
         out_ref[:, :, lanes] = res.astype(jnp.bfloat16).reshape(chans, tile, chunk)
 
 
@@ -216,18 +224,61 @@
     return jnp.stack([s[0] * g[0] + s[1] * g[1], s[0] * g[1] - s[1] * g[0]])
 
 
-def scatter_sum(terms, n_gx, n_gy):
-    two, chans = terms.shape[:2]
-    own_k, own_m = MY // n_gx, MX // n_gy
-    blocks = terms.reshape(two, chans, n_gx, own_k, n_gy, own_m).transpose(2, 4, 0, 1, 3, 5)
-    blocks = blocks.reshape(n_gx * n_gy, two, chans, own_k, own_m)
-    got = lax.all_to_all(blocks, ("gx", "gy"), split_axis=0, concat_axis=0, tiled=True)
-    return got.astype(jnp.float32).sum(axis=0)
-
-
-def gather_modes(modes):
-    along = lax.all_gather(modes, "gy", axis=3, tiled=True)
-    return lax.all_gather(along, "gx", axis=2, tiled=True)
+def bits_of(size):
+    return range(size.bit_length() - 1)
+
+
+def swap(array, axis, size, distance):
+    return lax.ppermute(array, axis, [(i, i ^ distance) for i in range(size)])
+
+
+def halve(array, axis, size, dim, beside):
+    for b in bits_of(size):
+        bit = (lax.axis_index(axis) >> b) & 1
+        shape = array.shape
+        split = array.reshape(shape[:dim] + (shape[dim] // 2, 2) + shape[dim + 1:])
+        keep, send = (
+            lax.dynamic_index_in_dim(split, which, dim + 1, False) for which in (bit, 1 - bit)
+        )
+        got = swap(send, axis, size, 1 << b)
+        if b == 0 and beside is not None:
+            got, beside = lax.optimization_barrier((got, beside))
+        total = keep.astype(jnp.float32) + got.astype(jnp.float32)
+        array = total.astype(jnp.bfloat16)
+    return total, beside
+
+
+def double(array, axis, size, dim):
+    for b in reversed(bits_of(size)):
+        first = ((lax.axis_index(axis) >> b) & 1) == 0
+        got = swap(array, axis, size, 1 << b)
+        both = jnp.stack([jnp.where(first, array, got), jnp.where(first, got, array)], dim + 1)
+        shape = array.shape
+        array = both.reshape(shape[:dim] + (2 * shape[dim],) + shape[dim + 1:])
+    return array
+
+
+def scatter_sum(terms, n_gx, n_gy, beside=(None, None)):
+    chans, wide = terms.shape[1], terms.shape[3]
+    total, one = halve(terms, "gy", n_gy, 0, beside[0])
+    total = total.astype(jnp.bfloat16)[0].reshape(chans, n_gx, MY // n_gx, wide)
+    total, two = halve(total, "gx", n_gx, 1, beside[1])
+    total = total[:, 0]
+    return jnp.stack([total[:, :, :wide // 2], total[:, :, wide // 2:]]), (one, two)
+
+
+def gather_modes(modes, n_gx, n_gy):
+    packed = jnp.concatenate([modes[0], modes[1]], -1)
+    chans, _, wide = packed.shape
+    packed = double(packed[:, None], "gx", n_gx, 1).reshape(1, chans, MY, wide)
+    return double(packed, "gy", n_gy, 0)
+
+
+def total_sum(array, n_gx, n_gy):
+    for axis, size in (("gx", n_gx), ("gy", n_gy)):
+        for b in bits_of(size):
+            array = array + swap(array, axis, size, 1 << b)
+    return array
 
 
 def on_device(n_gx, n_gy, state_in, tile_class, class_bias, w_point, spec_weight, grad_out):
@@ -237,18 +288,22 @@
     gy_index = lax.axis_index("gy")
     col_index = lax.axis_index("col")
     bf16 = jnp.bfloat16
-    y_all, x_all = host_tables()
+    y_all, x_all = host_tables(n_gy)
     y_table = lax.dynamic_slice_in_dim(jnp.asarray(y_all), gy_index * cols, cols, 1)
-    x_table = lax.dynamic_slice_in_dim(jnp.asarray(x_all), gx_index * rows, rows, 0)
-    x_table_t = lax.dynamic_slice_in_dim(jnp.asarray(x_all.T.copy()), gx_index * rows, rows, 1)
-    state_all = lax.all_gather(state_in, "col", axis=0, tiled=True)
+    x_table = lax.dynamic_slice_in_dim(jnp.asarray(x_all), gx_index * rows, rows, 1)
+    x_table_t = lax.dynamic_slice_in_dim(jnp.asarray(x_all.transpose(0, 2, 1).copy()), gx_index * rows, rows, 2)
+    state_other = swap(state_in, "col", 2, 1)
+    first = col_index == 0
     w_rows = lax.dynamic_slice_in_dim(w_point, col_index * chans, chans, 0)
     w_cols = lax.dynamic_slice_in_dim(w_point, col_index * chans, chans, 1)
     same = jnp.eye(TILE, dtype=bf16)
-    kron_fwd = (w_rows[:, None, :, None] * same[None, :, None, :]).reshape(chans * TILE, every * TILE)
-    kron_bwd = (w_cols.T[:, None, :, None] * same[None, :, None, :]).reshape(
-        chans * TILE, every * TILE
-    )
+    def kron_pair(weight):
+        halves = weight.reshape(chans, 2, chans).transpose(1, 0, 2)
+        halves = jnp.where(first, halves, halves[::-1])
+        spread = halves[:, :, None, :, None] * same[None, None, :, None, :]
+        return spread.reshape(2, chans * TILE, chans * TILE)
+
+    kron_fwd, kron_bwd = kron_pair(w_rows), kron_pair(w_cols.T)
     hot = (
         jnp.repeat(tile_class, TILE, axis=1)[:, None, :]
         == (jnp.arange(2 * NCLASS, dtype=jnp.int32) % NCLASS)[None, :, None]
@@ -262,62 +317,70 @@
     cells = rows * cols
     wide = 2 * MY
     block = pl.BlockSpec((chans, TILE, cols), lambda b: (0, b, 0))
-    block_all = pl.BlockSpec((every, TILE, cols), lambda b: (0, b, 0))
     block_hot = pl.BlockSpec((1, 2 * NCLASS, cols), lambda b: (b, 0, 0))
-    modes_shape = jax.ShapeDtypeStruct((2, chans, MY, MX), bf16)
+    modes_shape = jax.ShapeDtypeStruct((n_gy, chans, MY, wide // n_gy), bf16)
     field_shape = jax.ShapeDtypeStruct((chans, rows, cols), bf16)
     rows_scratch = pltpu.VMEM((chans, rows, wide), bf16)
 
     terms = call(
         fwd_kernel, "forward_transform", (chans,),
         [pl.BlockSpec((1, rows, cols), lambda c: (c, 0, 0)), whole(y_table), whole(x_table)],
-        pl.BlockSpec((2, 1, MY, MX), lambda c: (0, c, 0, 0)),
+        pl.BlockSpec((n_gy, 1, MY, wide // n_gy), lambda c: (0, c, 0, 0)),
         modes_shape, [], (2 * chans * cells * wide, 2 * chans * cells),
     )(state_in, y_table, x_table)
-    spectrum = scatter_sum(terms, n_gx, n_gy) * SCALE_FWD
+    spectrum = scatter_sum(terms, n_gx, n_gy)[0] * SCALE_FWD
     spec_all = lax.all_gather(spectrum, "col", axis=1, tiled=True)
     weight_f = spec_weight.astype(jnp.float32)
     mixed = mix_modes(weight_f, spec_all).astype(bf16)
-    mixed_all = gather_modes(mixed)
+    mixed_all = gather_modes(mixed, n_gx, n_gy)
 
     act_out, grad_pre, grad_terms = call(
         mid_kernel, "layer_and_adjoint", (steps,),
-        [block_all, block, whole(modes_shape), whole(kron_fwd), whole(y_table), whole(x_table),
+        [block, block, block, whole(modes_shape), whole(kron_fwd), whole(y_table), whole(x_table),
          whole(x_table_t), whole(bias_pair), block_hot],
         [block, block, whole(modes_shape)],
         [field_shape, field_shape, modes_shape],
         [rows_scratch, rows_scratch],
         (2 * chans * cells * (2 * wide + every * TILE), 10 * chans * cells),
-    )(state_all, grad_out, mixed_all, kron_fwd, y_table, x_table, x_table_t, bias_pair, hot)
-
-    grad_all = lax.all_gather(grad_pre, "col", axis=0, tiled=True)
-    point_sum, bias_sum = call(
-        sums_kernel, "weight_sums", (steps,), [block_all, block, block_hot],
-        [pl.BlockSpec((chans, every), lambda b: (0, 0)),
-         pl.BlockSpec((chans, 2 * NCLASS), lambda b: (0, 0))],
-        [jax.ShapeDtypeStruct((chans, every), jnp.float32),
-         jax.ShapeDtypeStruct((chans, 2 * NCLASS), jnp.float32)],
-        [pltpu.VMEM((chans * TILE, every * TILE), jnp.float32),
-         pltpu.VMEM((chans, 2 * NCLASS), jnp.float32)],
-        (2 * chans * cells * every * TILE, 6 * chans * cells),
-    )(state_all, grad_pre, hot)
-    sums = jnp.concatenate([point_sum, bias_sum], 1)
-    sums = lax.all_gather(sums, ("gx", "gy"), axis=0, tiled=False).sum(axis=0)
-    point_grad = sums[:, :every]
+    )(state_in, state_other, grad_out, mixed_all, kron_fwd, y_table, x_table, x_table_t, bias_pair, hot)
+
+    grad_other = swap(grad_pre, "col", 2, 1)
+    def half_sums(part):
+        start = part * (steps // 2)
+        some = pl.BlockSpec((chans, TILE, cols), lambda b: (0, start + b, 0))
+        some_hot = pl.BlockSpec((1, 2 * NCLASS, cols), lambda b: (start + b, 0, 0))
+        point_sum, bias_sum = call(
+            sums_kernel, f"weight_sums_{part}", (steps // 2,), [some, some, some, some_hot],
+            [pl.BlockSpec((chans, every), lambda b: (0, 0)),
+             pl.BlockSpec((chans, 2 * NCLASS), lambda b: (0, 0))],
+            [jax.ShapeDtypeStruct((chans, every), jnp.float32),
+             jax.ShapeDtypeStruct((chans, 2 * NCLASS), jnp.float32)],
+            [pltpu.VMEM((chans * TILE, every * TILE), jnp.float32),
+             pltpu.VMEM((chans, 2 * NCLASS), jnp.float32)],
+            (chans * cells * every * TILE, 3 * chans * cells),
+        )(state_in, state_other, grad_pre, hot)
+        return jnp.concatenate([point_sum, bias_sum], 1)
+
+    grad_modes, halves = scatter_sum(grad_terms, n_gx, n_gy, (half_sums(0), half_sums(1)))
+    sums = halves[0] + halves[1]
+    sums = total_sum(sums, n_gx, n_gy)
+    own, other = sums[:, :chans], sums[:, chans:every]
+    point_grad = jnp.concatenate(
+        [jnp.where(first, own, other), jnp.where(first, other, own)], 1
+    )
     bias_grad = sums[:, every:every + NCLASS].T
 
-    grad_modes = scatter_sum(grad_terms, n_gx, n_gy)
     input_terms = back_mix(weight_f, grad_modes)
     input_modes = lax.psum_scatter(input_terms, "col", scatter_dimension=1, tiled=True).astype(bf16)
-    input_all = gather_modes(input_modes)
+    input_all = gather_modes(input_modes, n_gx, n_gy)
     spec_grad = weight_grad(spec_all, grad_modes)
 
     grad_in = call(
         back_kernel, "input_gradient", (steps,),
-        [block_all, whole(modes_shape), whole(kron_bwd), whole(y_table), whole(x_table)],
+        [block, block, whole(modes_shape), whole(kron_bwd), whole(y_table), whole(x_table)],
         block, field_shape, [rows_scratch],
         (2 * chans * cells * (wide + every * TILE), 6 * chans * cells),
-    )(grad_all, input_all, kron_bwd, y_table, x_table)
+    )(grad_pre, grad_other, input_all, kron_bwd, y_table, x_table)
     return (act_out, grad_in, spec_grad, point_grad, bias_grad)
 
 

time: 452 us -> 308 us (0.68)
  blocking collectives: 128 us -> 2.56 us
  local copies, waits for them, and re-layouts: 44.2 us -> 22.1 us
  waiting for transfers between devices: 78.3 us -> 61.1 us
  starting transfers between devices: 0.6 us -> 16.8 us
    all_gather x4 -> x0, waiting for transfers between devices: 70.2 us -> none  [the longest x1 52.3 us: on_device(): state_all = lax.all_gather(state_in, 'col', axis=0, tiled=True)]
    all_to_all x2 -> x0, blocking collectives: 65.2 us -> none  [scatter_sum(): lax.all_to_all(blocks, ('gx', 'gy'), split_axis=0, concat_axis=0, tiled=T...]
    ppermute x0 -> x17, waiting for transfers between devices: none -> 61 us  [swap(): return lax.ppermute(array, axis, [(i, i ^ distance) for i in range(size)])]
    all_gather x3 -> x0, blocking collectives: 60.3 us -> none  [the longest x1 30.8 us: on_device(): sums = lax.all_gather(sums, ('gx', 'gy'), axis=0, tiled=False).sum(axis=0)]
    ppermute x0 -> x17, starting transfers between devices: none -> 16.8 us  [swap(): return lax.ppermute(array, axis, [(i, i ^ distance) for i in range(size)])]
    unnamed x30 -> x21, local copies, waits for them, and re-layouts: 17.3 us -> 3.97 us
    unnamed x6 -> x2, waiting for transfers between devices: 8.15 us -> 0.02 us
    reshape x4 -> x2, local copies, waits for them, and re-layouts: 7.62 us -> 0.17 us  [kron_pair(): halves = weight.reshape(chans, 2, chans).transpose(1, 0, 2)]
  transfers between devices with their start and end apart: 5 -> 18, of which waited for: 3 -> 10; matrix products, arithmetic and copies ran while one was open for 7% -> 19% of each run, Pallas kernels for 8% -> 17%
where the time goes in v2:
time: 308 us; the launch traced here: 304 us
  Pallas kernels  151 us (49%)
  waiting for transfers between devices  61.1 us (20%)
  other arithmetic  36.2 us (12%)
  local copies, waits for them, and re-layouts  22.1 us (7%)
  starting transfers between devices  16.8 us (5%)
  between operations  14.5 us (5%)
    pallas_call x1, Pallas kernels, on_device(): call(mid_kernel, 'layer_and_adjoint', (steps,), [block, block, block, who...  61.5 us
    ppermute x17, waiting for transfers between devices, swap(): return lax.ppermute(array, axis, [(i, i ^ distance) for i in range(size)])  61 us
    pallas_call x1, Pallas kernels, on_device(): call(back_kernel, 'input_gradient', (steps,), [block, block, whole(modes_...  37 us
    pallas_call x2, Pallas kernels, half_sums(): call(sums_kernel, f'weight_sums_{part}', (steps // 2,), [some, some, some...  35.4 us
    pallas_call x1, Pallas kernels, on_device(): call(fwd_kernel, 'forward_transform', (chans,), [pl.BlockSpec((1, rows, c...  17.1 us
    ppermute x17, starting transfers between devices, swap(): return lax.ppermute(array, axis, [(i, i ^ distance) for i in range(size)])  16.8 us
    mul x6, local copies, waits for them, and re-layouts, kron_pair(): spread = halves[:, :, None, :, None] * same[None, None, :, None, :]  11.6 us
    another operation x1, other arithmetic, weight_grad(): return jnp.stack([s[0] * g[0] + s[1] * g[1], s[0] * g[1] - s[1] * g[0]])  10.1 us
  transfers between devices with their start and end apart: 18, of which 10 were waited for; matrix products, arithmetic and copies ran while one was open for 19% of the time, Pallas kernels for 17%

profile of v2, /device:TPU:0, one launch (start us, length us, event | category | flops | bytes accessed | tf_op | source)
XLA Modules:
  0.0 304.2 jit_solution(11474445808340043856)
XLA Ops:
  7.7 1.1 constant_dynamic-slice_fusion.9.y_ref
  8.8 1.1 constant_dynamic-slice_fusion.8.x_ref
  9.9 17.1 %forward_transform.1 = bf16[2,16,128,128]{3,2,1,0:T(8,128)(2,1)S(1)} custom-call(bf16[16,512,1024]{2,1,0:T(8,128)(2,1)} %state_ref.7, bf16[256,1024]{1,0:T(8,128)(2,1)S(1)} %constant_dynamic-slice_fusion.9.y_ref, bf16[2,512,256]{2,1,0:T(8,128)(2,1)S(1)} %constant_dynamic-slice_fusion.8.x_ref), custom_call_target="tpu_custom_call" | custom-call | flops 4294967296 | bytes 16777216 | tf_op jit(solution)/shard_map/forward_transform/pallas_call | solution.py:325
  27.1 2.5 collective-permute-start.1
  29.7 12.6 %collective-permute-done.1 = bf16[1,16,128,128]{3,2,1,0:T(8,128)(2,1)S(1)} collective-permute-done((bf16[1,16,128,128]{3,2,1,0:T(8,128)(2,1)S(1)}, bf16[1,16,128,128]{3,2,1,0:T(8,128)(2,1)S(1)}, u32[]{:S(2)}, u32[]{:S(2)}) %collective-permute-start.1) | collective-permute-done | bytes 524320 | tf_op jit(solution)/shard_map/ppermute | solution.py:232
  42.4 1.9 collective-permute-start.2
  44.5 6.1 %collective-permute-done.2 = bf16[16,2,32,128]{3,2,1,0:T(8,128)(2,1)S(1)} collective-permute-done((bf16[16,2,32,128]{3,2,1,0:T(8,128)(2,1)S(1)}, bf16[16,2,32,128]{3,2,1,0:T(8,128)(2,1)S(1)}, u32[]{:S(2)}, u32[]{:S(2)}) %collective-permute-start.2) | collective-permute-done | bytes 262176 | tf_op jit(solution)/shard_map/ppermute | solution.py:232
  50.7 2.7 collective-permute-start.3
  53.5 5.4 %collective-permute-done.3 = bf16[16,1,32,128]{3,2,1,0:T(8,128)(2,1)S(1)} collective-permute-done((bf16[16,1,32,128]{3,2,1,0:T(8,128)(2,1)S(1)}, bf16[16,1,32,128]{3,2,1,0:T(8,128)(2,1)S(1)}, u32[]{:S(2)}, u32[]{:S(2)}) %collective-permute-start.3) | collective-permute-done | bytes 131104 | tf_op jit(solution)/shard_map/ppermute | solution.py:232
  59.2 2.6 all_gather.3
  61.7 1.2 slice_bitcast_fusion.3
  63.0 6.3 %fusion.2 = (f32[32,64,16]{1,0,2:T(8,128)S(1)}, f32[32,64,16]{1,0,2:T(8,128)S(1)}, f32[32,64,16]{1,0,2:T(8,128)S(1)}, f32[32,64,16]{1,0,2:T(8,128)S(1)}) fusion(f32[32,64,32]{1,0,2:T(8,128)S(1)} %get-tuple-element.60, bf16[2,32,16,32,64]{4,3,2,1,0:T(8,128)(2,1)} %param.13, f32[32,64,32]{1,0,2:T(8,128)S(1)} %get-tuple-element.59), kind=kLoop, calls=%fused_computation.11 | loop fusion | flops 10354688 | bytes 5242880 | tf_op jit(solution)/shard_map/iokm,ikm->okm/dot_general | solution.py:202
  70.0 1.1 constant_dynamic-slice_fusion.4.xt_ref
  71.1 7.7 %collective-permute-done.4 = bf16[16,1,32,128]{3,2,0,1:T(8,128)(2,1)S(1)} collective-permute-done((bf16[16,1,32,128]{3,2,0,1:T(8,128)(2,1)S(1)}, bf16[16,1,32,128]{3,2,0,1:T(8,128)(2,1)S(1)}, u32[]{:S(2)}, u32[]{:S(2)}) %collective-permute-start.4) | collective-permute-done | bytes 131104 | tf_op jit(solution)/shard_map/ppermute | solution.py:232
  79.4 7.2 %collective-permute-done.5 = bf16[16,2,32,128]{3,2,0,1:T(8,128)(2,1)S(1)} collective-permute-done((bf16[16,2,32,128]{3,2,0,1:T(8,128)(2,1)S(1)}, bf16[16,2,32,128]{3,2,0,1:T(8,128)(2,1)S(1)}, u32[]{:S(2)}, u32[]{:S(2)}) %collective-permute-start.5) | collective-permute-done | bytes 262176 | tf_op jit(solution)/shard_map/ppermute | solution.py:232
  86.8 1.3 collective-permute-start.6
  88.6 1.7 mul.141
  90.3 3.9 %mul.142 = bf16[2,256,256]{2,1,0:T(8,128)(2,1)} reshape(bf16[2,16,16,16,16]{4,3,2,1,0:T(8,128)(2,1)} %mul.141) | data formatting | bytes 524288 | tf_op jit(solution)/shard_map/mul | solution.py:303
  94.3 1.0 mul.138
  95.3 1.7 mul.135
  97.0 3.2 %mul.136 = bf16[2,256,256]{2,1,0:T(8,128)(2,1)S(1)} reshape(bf16[2,16,16,16,16]{4,3,2,1,0:T(8,128)(2,1)} %mul.135) | data formatting | bytes 524288 | tf_op jit(solution)/shard_map/mul | solution.py:303
  100.2 0.8 copy.36
  101.2 1.0 broadcast_multiply_fusion
  102.2 1.9 compare_convert_fusion.hot_ref
  104.1 1.1 select_bitcast_fusion.3
  105.4 61.5 %layer_and_adjoint.1 = (bf16[16,512,1024]{2,1,0:T(8,128)(2,1)}, bf16[16,512,1024]{2,1,0:T(8,128)(2,1)}, bf16[2,16,128,128]{3,2,1,0:T(8,128)(2,1)S(1)}) custom-call(bf16[16,512,1024]{2,1,0:T(8,128)(2,1)} %state_ref.7, bf16[16,512,1024]{2,1,0:T(8,128)(2,1)} %collective-permute-done.other_ref, bf16[16,512,1024]{2,1,0:T(8,128)(2,1)} %gout_ref.1, ...), custom_call_target="tpu_custom_call" | custom-call | flops 17179869184 | bytes 83886080 | tf_op jit(solution)/shard_map/layer_and_adjoint/pallas_call | solution.py:337
  167.0 0.9 collective-permute-start.8
  167.8 17.3 %weight_sums_0.1 = (f32[16,32]{1,0:T(8,128)S(1)}, f32[16,16]{1,0:T(8,128)S(1)}) custom-call(bf16[16,512,1024]{2,1,0:T(8,128)(2,1)} %state_ref.7, bf16[16,512,1024]{2,1,0:T(8,128)(2,1)} %collective-permute-done.other_ref, bf16[16,512,1024]{2,1,0:T(8,128)(2,1)} %get-tuple-element.17.gpre_ref.grad_ref, bf16[32,16,1024]{2,1,0:T(8,128)(2,1)S(1)} %copy-done.2), custom_call_target="tpu_custom_call" | custom-call | flops 4294967296 | bytes 25165824 | tf_op jit(solution)/shard_map/weight_sums_0/pallas_call | solution.py:352
  185.8 18.1 %weight_sums_1.1 = (f32[16,32]{1,0:T(8,128)S(1)}, f32[16,16]{1,0:T(8,128)S(1)}) custom-call(bf16[16,512,1024]{2,1,0:T(8,128)(2,1)} %state_ref.7, bf16[16,512,1024]{2,1,0:T(8,128)(2,1)} %collective-permute-done.other_ref, bf16[16,512,1024]{2,1,0:T(8,128)(2,1)} %get-tuple-element.17.gpre_ref.grad_ref, bf16[32,16,1024]{2,1,0:T(8,128)(2,1)S(1)} %copy-done.2), custom_call_target="tpu_custom_call" | custom-call | flops 4294967296 | bytes 25165824 | tf_op jit(solution)/shard_map/weight_sums_1/pallas_call | solution.py:352
  204.1 2.1 collective-permute-start.10
  206.2 7.1 %collective-permute-done.10 = bf16[16,1,32,128]{3,2,1,0:T(8,128)(2,1)S(1)} collective-permute-done((bf16[16,1,32,128]{3,2,1,0:T(8,128)(2,1)S(1)}, bf16[16,1,32,128]{3,2,1,0:T(8,128)(2,1)S(1)}, u32[]{:S(2)}, u32[]{:S(2)}) %collective-permute-start.10) | collective-permute-done | bytes 131104 | tf_op jit(solution)/shard_map/ppermute | solution.py:232
  213.4 0.9 fusion.14
  214.3 5.8 %fusion.6 = (f32[32,64,32]{1,0,2:T(8,128)S(1)}, f32[32,64,32]{1,0,2:T(8,128)S(1)}, f32[32,64,32]{1,0,2:T(8,128)S(1)}, f32[32,64,32]{1,0,2:T(8,128)S(1)}) fusion(f32[32,64,16]{1,0,2:T(8,128)S(1)} %get-tuple-element.72, bf16[2,32,16,32,64]{4,3,2,1,0:T(8,128)(2,1)S(1)} %bitcast.164, f32[32,64,16]{1,0,2:T(8,128)S(1)} %get-tuple-element.71), kind=kLoop, calls=%fused_computation.15 | loop fusion | flops 10223616 | bytes 5505024 | tf_op jit(solution)/shard_map/iokm,okm->ikm/dot_general | solution.py:212
  220.4 1.2 reshape.142
  221.7 3.6 %collective-permute-done.14 = f32[16,48]{1,0:T(8,128)S(1)} collective-permute-done((f32[16,48]{1,0:T(8,128)S(1)}, f32[16,48]{1,0:T(8,128)S(1)}, u32[]{:S(2)}, u32[]{:S(2)}) %collective-permute-start.14) | collective-permute-done | bytes 3104 | tf_op jit(solution)/shard_map/ppermute | solution.py:232
  225.3 0.6 collective-permute-start.15
  225.9 4.0 %collective-permute-done.15 = f32[16,48]{1,0:T(8,128)S(1)} collective-permute-done((f32[16,48]{1,0:T(8,128)S(1)}, f32[16,48]{1,0:T(8,128)S(1)}, u32[]{:S(2)}, u32[]{:S(2)}) %collective-permute-start.15) | collective-permute-done | bytes 3104 | tf_op jit(solution)/shard_map/ppermute | solution.py:232
  229.9 1.2 collective-permute-start.16
  231.1 2.4 collective-permute-done.16
  233.6 1.2 reshape.143
  235.0 0.6 collective-permute-start.11
  235.7 0.7 copy.41
  236.4 0.7 pad_maximum_fusion.6
  237.0 4.8 %collective-permute-done.11 = bf16[16,1,32,128]{3,2,0,1:T(8,128)(2,1)S(1)} collective-permute-done((bf16[16,1,32,128]{3,2,0,1:T(8,128)(2,1)S(1)}, bf16[16,1,32,128]{3,2,0,1:T(8,128)(2,1)S(1)}, u32[]{:S(2)}, u32[]{:S(2)}) %collective-permute-start.11) | collective-permute-done | bytes 131104 | tf_op jit(solution)/shard_map/ppermute | solution.py:232
  242.2 6.4 %multiply_add_fusion = (f32[1,32,16,32,64]{4,3,2,1,0:T(8,128)S(1)}, f32[1,32,16,32,64]{4,3,2,1,0:T(8,128)}) fusion(f32[16,32,64]{2,1,0:T(8,128)} %get-tuple-element.73, f32[32,32,64]{2,1,0:T(8,128)S(1)} %copy-done.4, f32[16,32,64]{2,1,0:T(8,128)} %get-tuple-element.70, f32[32,32,64]{2,1,0:T(8,128)S(1)} %copy-done.3), kind=kLoop, calls=%fused_computation.18 | loop fusion | flops 6291456 | bytes 9175040 | tf_op jit(solution)/shard_map/add | solution.py:224
  248.7 1.3 collective-permute-start.13
  250.0 10.1 %pad_maximum_fusion = f32[2,32,16,32,64]{4,3,2,1,0:T(8,128)} fusion(f32[1,32,16,32,64]{4,3,2,1,0:T(8,128)} %get-tuple-element.57, f32[1,32,16,32,64]{4,3,2,1,0:T(8,128)S(1)} %get-tuple-element.56), kind=kLoop, calls=%fused_computation | loop fusion | flops 2097152 | bytes 16777216 | tf_op jit(solution)/shard_map/stack | solution.py:224
  260.3 37.0 %input_gradient.1 = bf16[16,512,1024]{2,1,0:T(8,128)(2,1)} custom-call(bf16[16,512,1024]{2,1,0:T(8,128)(2,1)} %get-tuple-element.17.gpre_ref.grad_ref, bf16[16,512,1024]{2,1,0:T(8,128)(2,1)} %collective-permute-done.7.other_ref, bf16[2,16,128,128]{3,2,1,0:T(8,128)(2,1)S(1)} %maximum_bitcast_fusion.1.modes_ref, ...), custom_call_target="tpu_custom_call" | custom-call | flops 12884901888 | bytes 50331648 | tf_op jit(solution)/shard_map/input_gradient/pallas_call | solution.py:378
  (94 shorter events, 6.0 us)
Async XLA Ops:
  7.2 46.3 %copy-start = (bf16[32,32]{1,0:T(8,128)(2,1)S(1)}, bf16[32,32]{1,0:T(8,128)(2,1)}, u32[]{:S(2)}) copy-start(bf16[32,32]{1,0:T(8,128)(2,1)} %param.12) | copy-start | bytes 6148
  7.2 226.5 %reduce-scatter.4.cloned.1.call-start = ((), (), s32[]{:S(2)}) async-start(), calls=%async_computation.1 | async-start | bytes 786432
  7.2 98.1 %collective-permute-start = (bf16[16,512,1024]{2,1,0:T(8,128)(2,1)}, bf16[16,512,1024]{2,1,0:T(8,128)(2,1)}, u32[]{:S(2)}, u32[]{:S(2)}) collective-permute-start(bf16[16,512,1024]{2,1,0:T(8,128)(2,1)} %state_ref.7), channel_id=1, source_target_pairs={{0,1},{1,0},{2,3},{3,2},{4,5},{5,4},{6,7},{7,6},{8,9},{9,8},{10,11... | collective-permute-start | bytes 50331656 | tf_op jit(solution)/shard_map/ppermute | solution.py:232
  9.9 34.4 %copy-start.5 = (f32[8,32]{1,0:T(8,128)S(1)}, f32[8,32]{1,0:T(8,128)}, u32[]{:S(2)}) copy-start(f32[8,32]{1,0:T(8,128)} %param.11) | copy-start | bytes 3076
  27.1 15.1 %collective-permute-start.1 = (bf16[1,16,128,128]{3,2,1,0:T(8,128)(2,1)S(1)}, bf16[1,16,128,128]{3,2,1,0:T(8,128)(2,1)S(1)}, u32[]{:S(2)}, u32[]{:S(2)}) collective-permute-start(bf16[1,16,128,128]{3,2,1,0:T(8,128)(2,1)S(1)} %constant_dynamic-slice_fusion.7), channel_id=1, source_target_pairs={{0,2},{2,0},{1,3},{3,1},{4,6},{6,4},{5,7},{7,5},{8,10},{10,8},{9,1... | collective-permute-start | bytes 1572872 | tf_op jit(solution)/shard_map/ppermute | solution.py:232
  42.4 8.2 %collective-permute-start.2 = (bf16[16,2,32,128]{3,2,1,0:T(8,128)(2,1)S(1)}, bf16[16,2,32,128]{3,2,1,0:T(8,128)(2,1)S(1)}, u32[]{:S(2)}, u32[]{:S(2)}) collective-permute-start(bf16[16,2,32,128]{3,2,1,0:T(8,128)(2,1)S(1)} %dynamic-slice_bitcast_fusion.1), channel_id=1, source_target_pairs={{0,4},{4,0},{8,12},{12,8},{1,5},{5,1},{9,13},{13,9},{2,6},{6,2},{1... | collective-permute-start | bytes 786440 | tf_op jit(solution)/shard_map/ppermute | solution.py:232
  50.7 8.2 %collective-permute-start.3 = (bf16[16,1,32,128]{3,2,1,0:T(8,128)(2,1)S(1)}, bf16[16,1,32,128]{3,2,1,0:T(8,128)(2,1)S(1)}, u32[]{:S(2)}, u32[]{:S(2)}) collective-permute-start(bf16[16,1,32,128]{3,2,1,0:T(8,128)(2,1)S(1)} %constant_dynamic-slice_fusion.6), channel_id=1, source_target_pairs={{0,8},{4,12},{8,0},{12,4},{1,9},{5,13},{9,1},{13,5},{2,10},{6,14},... | collective-permute-start | bytes 393224 | tf_op jit(solution)/shard_map/ppermute | solution.py:232
  69.5 9.3 %collective-permute-start.4 = (bf16[16,1,32,128]{3,2,0,1:T(8,128)(2,1)S(1)}, bf16[16,1,32,128]{3,2,0,1:T(8,128)(2,1)S(1)}, u32[]{:S(2)}, u32[]{:S(2)}) collective-permute-start(bf16[16,1,32,128]{3,2,0,1:T(8,128)(2,1)S(1)} %maximum_bitcast_fusion.4), channel_id=1, source_target_pairs={{0,8},{4,12},{8,0},{12,4},{1,9},{5,13},{9,1},{13,5},{2,10},{6,14},... | collective-permute-start | bytes 393224 | tf_op jit(solution)/shard_map/ppermute | solution.py:232
  79.0 7.7 %collective-permute-start.5 = (bf16[16,2,32,128]{3,2,0,1:T(8,128)(2,1)S(1)}, bf16[16,2,32,128]{3,2,0,1:T(8,128)(2,1)S(1)}, u32[]{:S(2)}, u32[]{:S(2)}) collective-permute-start(bf16[16,2,32,128]{3,2,0,1:T(8,128)(2,1)S(1)} %maximum_bitcast_fusion.2), channel_id=1, source_target_pairs={{0,4},{4,0},{8,12},{12,8},{1,5},{5,1},{9,13},{13,9},{2,6},{6,2},{1... | collective-permute-start | bytes 786440 | tf_op jit(solution)/shard_map/ppermute | solution.py:232
  86.8 17.4 %collective-permute-start.6 = (bf16[1,16,128,128]{3,2,1,0:T(8,128)(2,1)S(1)}, bf16[1,16,128,128]{3,2,1,0:T(8,128)(2,1)}, u32[]{:S(2)}, u32[]{:S(2)}) collective-permute-start(bf16[1,16,128,128]{3,2,1,0:T(8,128)(2,1)S(1)} %bitcast.165), channel_id=1, source_target_pairs={{0,2},{2,0},{1,3},{3,1},{4,6},{6,4},{5,7},{7,5},{8,10},{10,8},{9,1... | collective-permute-start | bytes 1572872 | tf_op jit(solution)/shard_map/ppermute | solution.py:232
  105.4 62.4 %copy-start.2 = (bf16[32,16,1024]{2,1,0:T(8,128)(2,1)S(1)}, bf16[32,16,1024]{2,1,0:T(8,128)(2,1)}, u32[]{:S(2)}) copy-start(bf16[32,16,1024]{2,1,0:T(8,128)(2,1)} %compare_convert_fusion.hot_ref) | copy-start | bytes 3145732
  166.9 93.4 %collective-permute-start.7 = (bf16[16,512,1024]{2,1,0:T(8,128)(2,1)}, bf16[16,512,1024]{2,1,0:T(8,128)(2,1)}, u32[]{:S(2)}, u32[]{:S(2)}) collective-permute-start(bf16[16,512,1024]{2,1,0:T(8,128)(2,1)} %get-tuple-element.17.gpre_ref.grad_ref), channel_id=1, source_target_pairs={{0,1},{1,0},{2,3},{3,2},{4,5},{5,4},{6,7},{7,6},{8,9},{9,8},{10,11... | collective-permute-start | bytes 50331656 | tf_op jit(solution)/shard_map/ppermute | solution.py:232
  167.0 18.2 %collective-permute-start.8 = (bf16[1,16,128,128]{3,2,1,0:T(8,128)(2,1)S(1)}, bf16[1,16,128,128]{3,2,1,0:T(8,128)(2,1)S(1)}, u32[]{:S(2)}, u32[]{:S(2)}) collective-permute-start(bf16[1,16,128,128]{3,2,1,0:T(8,128)(2,1)S(1)} %constant_dynamic-slice_fusion.2), channel_id=1, source_target_pairs={{0,2},{2,0},{1,3},{3,1},{4,6},{6,4},{5,7},{7,5},{8,10},{10,8},{9,1... | collective-permute-start | bytes 1572872 | tf_op jit(solution)/shard_map/ppermute | solution.py:232
  185.3 28.9 %slice-start = ((s8[8388608]{0:T(1024)(128)(4,1)}), s8[4194304]{0:T(1024)(128)(4,1)S(1)}, s32[]{:S(2)}) async-start(s8[8388608]{0:T(1024)(128)(4,1)} %bitcast.163), calls=%async_computation.2 | async-start | bytes 8388608
  185.4 28.9 %slice-start.1 = ((s8[8388608]{0:T(1024)(128)(4,1)}), s8[4194304]{0:T(1024)(128)(4,1)S(1)}, s32[]{:S(2)}) async-start(s8[8388608]{0:T(1024)(128)(4,1)} %bitcast.163), calls=%async_computation.3 | async-start | bytes 8388608
  185.4 18.5 %collective-permute-start.9 = (bf16[16,2,32,128]{3,2,1,0:T(8,128)(2,1)S(1)}, bf16[16,2,32,128]{3,2,1,0:T(8,128)(2,1)S(1)}, u32[]{:S(2)}, u32[]{:S(2)}) collective-permute-start(bf16[16,2,32,128]{3,2,1,0:T(8,128)(2,1)S(1)} %dynamic-slice_bitcast_fusion), channel_id=1, source_target_pairs={{0,4},{4,0},{8,12},{12,8},{1,5},{5,1},{9,13},{13,9},{2,6},{6,2},{1... | collective-permute-start | bytes 786440 | tf_op jit(solution)/shard_map/ppermute | solution.py:232
  204.1 9.3 %collective-permute-start.10 = (bf16[16,1,32,128]{3,2,1,0:T(8,128)(2,1)S(1)}, bf16[16,1,32,128]{3,2,1,0:T(8,128)(2,1)S(1)}, u32[]{:S(2)}, u32[]{:S(2)}) collective-permute-start(bf16[16,1,32,128]{3,2,1,0:T(8,128)(2,1)S(1)} %constant_dynamic-slice_fusion.1), channel_id=1, source_target_pairs={{0,8},{4,12},{8,0},{12,4},{1,9},{5,13},{9,1},{13,5},{2,10},{6,14},... | collective-permute-start | bytes 393224 | tf_op jit(solution)/shard_map/ppermute | solution.py:232
  214.3 27.9 %copy-start.3 = (f32[32,32,64]{2,1,0:T(8,128)S(1)}, f32[32,32,64]{2,1,0:T(8,128)}, u32[]{:S(2)}) copy-start(f32[32,32,64]{2,1,0:T(8,128)} %get-tuple-element.58) | copy-start | bytes 786436
  214.3 27.9 %copy-start.4 = (f32[32,32,64]{2,1,0:T(8,128)S(1)}, f32[32,32,64]{2,1,0:T(8,128)}, u32[]{:S(2)}) copy-start(f32[32,32,64]{2,1,0:T(8,128)} %get-tuple-element.61) | copy-start | bytes 786436
  221.6 3.7 %collective-permute-start.14 = (f32[16,48]{1,0:T(8,128)S(1)}, f32[16,48]{1,0:T(8,128)S(1)}, u32[]{:S(2)}, u32[]{:S(2)}) collective-permute-start(f32[16,48]{1,0:T(8,128)S(1)} %add.127), channel_id=1, source_target_pairs={{0,4},{4,0},{8,12},{12,8},{1,5},{5,1},{9,13},{13,9},{2,6},{6,2},{1... | collective-permute-start | bytes 9224 | tf_op jit(solution)/shard_map/ppermute | solution.py:232
  225.3 4.5 %collective-permute-start.15 = (f32[16,48]{1,0:T(8,128)S(1)}, f32[16,48]{1,0:T(8,128)S(1)}, u32[]{:S(2)}, u32[]{:S(2)}) collective-permute-start(f32[16,48]{1,0:T(8,128)S(1)} %add.128), channel_id=1, source_target_pairs={{0,8},{4,12},{8,0},{12,4},{1,9},{5,13},{9,1},{13,5},{2,10},{6,14},... | collective-permute-start | bytes 9224 | tf_op jit(solution)/shard_map/ppermute | solution.py:232
  229.9 3.7 %collective-permute-start.16 = (f32[16,48]{1,0:T(8,128)S(1)}, f32[16,48]{1,0:T(8,128)S(1)}, u32[]{:S(2)}, u32[]{:S(2)}) collective-permute-start(f32[16,48]{1,0:T(8,128)S(1)} %add.129), channel_id=1, source_target_pairs={{0,2},{2,0},{1,3},{3,1},{4,6},{6,4},{5,7},{7,5},{8,10},{10,8},{9,1... | collective-permute-start | bytes 9224 | tf_op jit(solution)/shard_map/ppermute | solution.py:232
  235.0 6.9 %collective-permute-start.11 = (bf16[16,1,32,128]{3,2,0,1:T(8,128)(2,1)S(1)}, bf16[16,1,32,128]{3,2,0,1:T(8,128)(2,1)S(1)}, u32[]{:S(2)}, u32[]{:S(2)}) collective-permute-start(bf16[16,1,32,128]{3,2,0,1:T(8,128)(2,1)S(1)} %maximum_bitcast_fusion.5), channel_id=1, source_target_pairs={{0,8},{4,12},{8,0},{12,4},{1,9},{5,13},{9,1},{13,5},{2,10},{6,14},... | collective-permute-start | bytes 393224 | tf_op jit(solution)/shard_map/ppermute | solution.py:232
  242.1 6.5 %collective-permute-start.12 = (bf16[16,2,32,128]{3,2,0,1:T(8,128)(2,1)S(1)}, bf16[16,2,32,128]{3,2,0,1:T(8,128)(2,1)S(1)}, u32[]{:S(2)}, u32[]{:S(2)}) collective-permute-start(bf16[16,2,32,128]{3,2,0,1:T(8,128)(2,1)S(1)} %maximum_bitcast_fusion.3), channel_id=1, source_target_pairs={{0,4},{4,0},{8,12},{12,8},{1,5},{5,1},{9,13},{13,9},{2,6},{6,2},{1... | collective-permute-start | bytes 786440 | tf_op jit(solution)/shard_map/ppermute | solution.py:232
  248.7 11.4 %collective-permute-start.13 = (bf16[1,16,128,128]{3,2,1,0:T(8,128)(2,1)S(1)}, bf16[1,16,128,128]{3,2,1,0:T(8,128)(2,1)S(1)}, u32[]{:S(2)}, u32[]{:S(2)}) collective-permute-start(bf16[1,16,128,128]{3,2,1,0:T(8,128)(2,1)S(1)} %bitcast.167), channel_id=1, source_target_pairs={{0,2},{2,0},{1,3},{3,1},{4,6},{6,4},{5,7},{7,5},{8,10},{10,8},{9,1... | collective-permute-start | bytes 1572872 | tf_op jit(solution)/shard_map/ppermute | solution.py:232
  260.3 37.1 %copy-start.1 = (bf16[32,32]{1,0:T(8,128)(2,1)S(1)}, bf16[32,32]{1,0:T(8,128)(2,1)}, u32[]{:S(2)}) copy-start(bf16[32,32]{1,0:T(8,128)(2,1)} %param.12) | copy-start | bytes 6148
Sparse Core Ops, SparseCore 0:
  221.7 7.5 reduce-scatter.3
